TPU v7x, 768 devices: a whole 4x8x12 slice. The times are simulated.
768 devices in a mesh: gx: 16 (over y, core), gy: 48 (over x, z).
Axes of the slice: x: 4, y: 8, z: 12, core: 2. Of those that a mesh axis runs over, the one named last changes fastest.
Arguments:
- atm_state: float32 [8, 1024, 6144], P(None, 'gx', 'gy'), may hold values from -6 to 6
- ocean_temp: float32 [10, 2048, 6144], P(None, 'gx', 'gy'), may hold values from -6 to 6
- flux_coef: float32 [12, 8], replicated, may hold values from -2 to 2
- flux_mix: float32 [10, 12], replicated, may hold values from -1.75 to 1.75
- intersect_share: bfloat16 [16, 4608, 128, 128], P('gx', 'gy'), may hold values from -0.5 to 0.5
- sender_tile_line: int32 [16, 4608], P('gx', 'gy'), may hold values from 0 to 63
- dest_tile_line: int32 [16, 4608], P('gx', 'gy'), may hold values from 0 to 127
- dst_owner: int32 [16, 4608, 1], P('gx', 'gy'), may hold values from 0 to 47; in each aligned block of 96 rows (0 to 95, 96 to 191, ..., all dimensions but the last counted through in order) at most 4 rows name the same one
Outputs:
- marine_final_heat: float32 [10, 2048, 6144], P(None, 'gx', 'gy')
- aerial_water_heat: float32 [1024, 6144], P('gx', 'gy')
Inputs may be any that keep to these rules, and one draw needn't show every extreme that they name: `dst_owner`: among the 96 blocks q with the same g and the same q // 96, no owner is named more than 4 times, a bound that some block reaches.
All inputs are finite; a program needn't handle non-finite values.
Results may differ from a plain program's by a relative error of at most 0.003.
Values may be sent and summed in bfloat16 or wider, within the bound.
A program may use at most 32 MiB of HBM per device.

v0:
```python
import jax
import jax.numpy as jnp
from jax import lax
from jax.sharding import PartitionSpec as P

diffusion_rate = 0.2
forcing_step = 0.5


def with_halo(block, sides, width):
    for axis, dim in sides:
        count = lax.axis_size(axis)
        forward = [(i, i + 1) for i in range(count - 1)]
        backward = [(target, source) for source, target in forward]
        low = lax.ppermute(
            lax.slice_in_dim(block, block.shape[dim] - width, None, axis=dim), axis, forward
        )
        high = lax.ppermute(lax.slice_in_dim(block, 0, width, axis=dim), axis, backward)
        block = jnp.concatenate([low, block, high], axis=dim)
    return block


def diffuse_once(padded):
    centre = padded[:, 1:-1, 1:-1]
    beside_all = (
        padded[:, :-2, 1:-1] + padded[:, 2:, 1:-1] + padded[:, 1:-1, :-2] + padded[:, 1:-1, 2:]
    )
    return centre + diffusion_rate * (beside_all - 4.0 * centre)


def atm_steps(field):
    for repeat in range(2):
        padded = with_halo(field, (("gx", 1), ("gy", 2)), 1)
        field = diffuse_once(padded)
    return field


def marine_step_count(field):
    for repeat in range(2):
        padded = with_halo(field, (("gx", 1), ("gy", 2)), 1)
        field = diffuse_once(padded)
    return field


def land_rows(value_entries, tile_ids, row_total):
    tile_hit = (jnp.arange(row_total, dtype=jnp.int32)[:, None] == tile_ids[None, :]).astype(
        jnp.float32
    )
    flat = value_entries.reshape(
        value_entries.shape[0], value_entries.shape[1] * value_entries.shape[2]
    )
    landed = jnp.dot(
        tile_hit, flat, precision=lax.Precision.HIGHEST, preferred_element_type=jnp.float32
    )
    return landed.reshape(row_total, value_entries.shape[1], value_entries.shape[2])


def place_slots(placing, value_entries, slot_count):
    flat = value_entries.reshape(
        value_entries.shape[0], value_entries.shape[1] * value_entries.shape[2]
    )
    placed = jnp.dot(
        placing.astype(jnp.float32),
        flat,
        precision=lax.Precision.HIGHEST,
        preferred_element_type=jnp.float32,
    )
    return placed.reshape(slot_count, value_entries.shape[1], value_entries.shape[2])


def body(
    atm_state,
    ocean_temp,
    flux_coef,
    flux_mix,
    intersect_share,
    sender_tile_line,
    dest_tile_line,
    dst_owner,
):
    peer_count = lax.axis_size("gy")
    block_count = sender_tile_line.shape[1]
    capacity = max(2, 2 * block_count // peer_count)
    slot_count = peer_count * capacity
    ocean_rows = ocean_temp.shape[1]
    atm_rows = atm_state.shape[1]
    atm_surface = atm_steps(atm_state)
    fluxes = jnp.tanh(
        jnp.einsum("kl,lxy->kxy", flux_coef, atm_surface, precision=lax.Precision.HIGHEST)
    ).astype(jnp.bfloat16)
    share_grid_array = intersect_share[0]
    src_row = sender_tile_line[0]
    tile_rows = jnp.take(fluxes, src_row, axis=1)
    contrib = jnp.einsum(
        "kqi,qio->qko", tile_rows, share_grid_array, preferred_element_type=jnp.float32
    )
    keeper_line = dst_owner[0, :, 0]
    owner_hit = (keeper_line[:, None] == jnp.arange(peer_count, dtype=jnp.int32)[None, :]).astype(
        jnp.int32
    )
    earlier = jnp.cumsum(owner_hit, axis=0) - owner_hit
    rank_in = jnp.sum(earlier * owner_hit, axis=1)
    place_finder = keeper_line * capacity + rank_in
    placing = jnp.arange(slot_count, dtype=jnp.int32)[:, None] == place_finder[None, :]
    send_ids = jnp.sum(jnp.where(placing, dest_tile_line[0][None, :] + 1, 0), axis=1) - 1
    send_values = place_slots(placing, contrib, slot_count)
    recv_values, arrived_slot_ids = (
        lax.all_to_all(send_values, "gy", split_axis=0, concat_axis=0, tiled=True),
        lax.all_to_all(send_ids, "gy", split_axis=0, concat_axis=0, tiled=True),
    )
    landed = land_rows(recv_values, arrived_slot_ids, ocean_rows)
    forcing = jnp.einsum("lk,xky->lxy", flux_mix, landed, precision=lax.Precision.HIGHEST)
    marine_initial_state = ocean_temp + forcing_step * forcing
    marine_final_heat = marine_step_count(marine_initial_state)
    skin_heat_field = marine_final_heat[0].astype(jnp.bfloat16)
    filled = arrived_slot_ids >= 0
    chosen_lines = jnp.take(skin_heat_field, jnp.maximum(arrived_slot_ids, 0), axis=0)
    send_back = jnp.where(filled[:, None], chosen_lines, jnp.zeros_like(chosen_lines))
    sent_home_amounts = lax.all_to_all(send_back, "gy", split_axis=0, concat_axis=0, tiled=True)
    tile_water_heat = jnp.take(sent_home_amounts, place_finder, axis=0)
    value_entries = jnp.einsum(
        "awq,aq->aw", share_grid_array, tile_water_heat, preferred_element_type=jnp.float32
    )
    src_hit = (jnp.arange(atm_rows, dtype=jnp.int32)[:, None] == src_row[None, :]).astype(
        jnp.float32
    )
    aerial_water_heat = jnp.dot(
        src_hit, value_entries, precision=lax.Precision.HIGHEST, preferred_element_type=jnp.float32
    )
    return (marine_final_heat, aerial_water_heat)


def solution(mesh):
    return jax.shard_map(
        body,
        mesh=mesh,
        in_specs=(
            P(None, "gx", "gy"),
            P(None, "gx", "gy"),
            P(),
            P(),
            P("gx", "gy", None, None),
            P("gx", "gy"),
            P("gx", "gy"),
            P("gx", "gy", None),
        ),
        out_specs=(P(None, "gx", "gy"), P("gx", "gy")),
        check_vma=False,
    )
```

profile of v0, /device:TPU:1, one launch (start us, length us, event | category | flops | bytes accessed | tf_op | source)
XLA Modules:
  0.0 238.8 jit_solution(3844584022513163802)
XLA Ops:
  0.7 0.9 fusion.66
  1.6 4.7 %collective-permute-start = (f32[8,1,128]{2,1,0:T(1,128)S(1)}, f32[8,1,128]{2,1,0:T(1,128)S(1)}, u32[]{:S(2)}, u32[]{:S(2)}) collective-permute-start(f32[8,1,128]{2,1,0:T(1,128)S(1)} %get-tuple-element.28), channel_id=1, source_target_pairs={{0,48},{48,96},{96,144},{144,192},{192,240},{240,288},{288,336},{3... | collective-permute-start | bytes 12296 | tf_op jit(solution)/shard_map/ppermute | solution.py:15
  6.3 9.1 %collective-permute-start.1 = (f32[8,1,128]{2,1,0:T(1,128)S(1)}, f32[8,1,128]{2,1,0:T(1,128)S(1)}, u32[]{:S(2)}, u32[]{:S(2)}) collective-permute-start(f32[8,1,128]{2,1,0:T(1,128)S(1)} %get-tuple-element.29), channel_id=1, source_target_pairs={{48,0},{96,48},{144,96},{192,144},{240,192},{288,240},{336,288},{3... | collective-permute-start | bytes 12296 | tf_op jit(solution)/shard_map/ppermute | solution.py:18
  16.1 0.7 fusion.51
  17.0 0.8 select_reduce_fusion.1
  18.6 0.7 sub.23
  19.4 11.0 %all-to-all-start = ((s32[48,4,1]{1,2,0:T(1,128)}), s32[48,4,1]{1,2,0:T(1,128)}, u32[]{:S(2)}, u32[]{:S(2)}) async-start(s32[48,4,1]{1,2,0:T(1,128)} %bitcast.2), calls=%async_computation | async-start | bytes 49152 | tf_op jit(solution)/shard_map/all_to_all | solution.py:109
  30.4 1.0 pad_maximum_fusion.18
  31.5 3.0 %collective-permute-start.2 = (f32[8,66,1]{2,1,0:T(8,128)S(1)}, f32[8,66,1]{2,1,0:T(8,128)S(1)}, u32[]{:S(2)}, u32[]{:S(2)}) collective-permute-start(f32[8,66,1]{2,1,0:T(8,128)S(1)} %get-tuple-element.24), channel_id=1, source_target_pairs={{0,1},{1,2},{2,3},{3,4},{4,5},{5,6},{6,7},{7,8},{8,9},{9,10},{10,1... | collective-permute-start | bytes 6344 | tf_op jit(solution)/shard_map/ppermute | solution.py:15
  34.5 1.3 collective-permute-start.3
  36.4 4.1 %collective-permute-done.2 = f32[8,66,1]{2,1,0:T(8,128)S(1)} collective-permute-done((f32[8,66,1]{2,1,0:T(8,128)S(1)}, f32[8,66,1]{2,1,0:T(8,128)S(1)}, u32[]{:S(2)}, u32[]{:S(2)}) %collective-permute-start.2) | collective-permute-done | bytes 2144 | tf_op jit(solution)/shard_map/ppermute | solution.py:15
  40.5 4.0 %collective-permute-done.3 = f32[8,66,1]{2,1,0:T(8,128)S(1)} collective-permute-done((f32[8,66,1]{2,1,0:T(8,128)S(1)}, f32[8,66,1]{2,1,0:T(8,128)S(1)}, u32[]{:S(2)}, u32[]{:S(2)}) %collective-permute-start.3) | collective-permute-done | bytes 2144 | tf_op jit(solution)/shard_map/ppermute | solution.py:18
  44.8 4.5 %collective-permute-start.4 = (f32[8,1,128]{2,1,0:T(1,128)S(1)}, f32[8,1,128]{2,1,0:T(1,128)S(1)}, u32[]{:S(2)}, u32[]{:S(2)}) collective-permute-start(f32[8,1,128]{2,1,0:T(1,128)S(1)} %get-tuple-element.26), channel_id=1, source_target_pairs={{0,48},{48,96},{96,144},{144,192},{192,240},{240,288},{288,336},{3... | collective-permute-start | bytes 12296 | tf_op jit(solution)/shard_map/ppermute | solution.py:15
  49.2 1.9 collective-permute-start.5
  51.2 3.0 %collective-permute-done.5 = f32[8,1,128]{2,1,0:T(1,128)S(1)} collective-permute-done((f32[8,1,128]{2,1,0:T(1,128)S(1)}, f32[8,1,128]{2,1,0:T(1,128)S(1)}, u32[]{:S(2)}, u32[]{:S(2)}) %collective-permute-start.5) | collective-permute-done | bytes 4128 | tf_op jit(solution)/shard_map/ppermute | solution.py:18
  54.4 3.1 %collective-permute-start.6 = (f32[8,66,1]{2,1,0:T(8,128)S(1)}, f32[8,66,1]{2,1,0:T(8,128)S(1)}, u32[]{:S(2)}, u32[]{:S(2)}) collective-permute-start(f32[8,66,1]{2,1,0:T(8,128)S(1)} %get-tuple-element.22), channel_id=1, source_target_pairs={{0,1},{1,2},{2,3},{3,4},{4,5},{5,6},{6,7},{7,8},{8,9},{9,10},{10,1... | collective-permute-start | bytes 6344 | tf_op jit(solution)/shard_map/ppermute | solution.py:15
  57.5 1.3 collective-permute-start.7
  58.8 4.1 %collective-permute-done.6 = f32[8,66,1]{2,1,0:T(8,128)S(1)} collective-permute-done((f32[8,66,1]{2,1,0:T(8,128)S(1)}, f32[8,66,1]{2,1,0:T(8,128)S(1)}, u32[]{:S(2)}, u32[]{:S(2)}) %collective-permute-start.6) | collective-permute-done | bytes 2144 | tf_op jit(solution)/shard_map/ppermute | solution.py:15
  62.9 4.5 %collective-permute-done.7 = f32[8,66,1]{2,1,0:T(8,128)S(1)} collective-permute-done((f32[8,66,1]{2,1,0:T(8,128)S(1)}, f32[8,66,1]{2,1,0:T(8,128)S(1)}, u32[]{:S(2)}, u32[]{:S(2)}) %collective-permute-start.7) | collective-permute-done | bytes 2144 | tf_op jit(solution)/shard_map/ppermute | solution.py:18
  67.7 1.4 fusion.10
  69.0 1.6 gather_fusion
  70.7 1.7 fusion.2
  72.3 0.8 fusion.24
  73.2 1.9 copy.55
  75.0 11.8 %all-to-all-start.1 = ((f32[192,12,128]{2,1,0:T(8,128)}), f32[192,12,128]{2,1,0:T(8,128)}, u32[]{:S(2)}, u32[]{:S(2)}) async-start(f32[192,12,128]{2,1,0:T(8,128)} %copy.55), calls=%async_computation.1 | async-start | bytes 3145728 | tf_op jit(solution)/shard_map/all_to_all | solution.py:108
  87.4 1.4 reduce.3
  88.9 56.3 %all-to-all-done.1 = f32[192,12,128]{2,1,0:T(8,128)} async-done(((f32[192,12,128]{2,1,0:T(8,128)}), f32[192,12,128]{2,1,0:T(8,128)}, u32[]{:S(2)}, u32[]{:S(2)}) %all-to-all-start.1) | async-done | bytes 1179680 | tf_op jit(solution)/shard_map/all_to_all | solution.py:108
  145.2 2.4 %fusion.7 = f32[128,12,128]{2,0,1:T(8,128)S(1)} fusion(s32[192]{0:T(256)S(1)} %eq.61, f32[24,8,12,128]{3,2,1,0:T(8,128)} %bitcast.33), kind=kOutput, calls=%fused_computation.13 | convolution fusion | flops 453009408 | bytes 1966848 | tf_op jit(solution)/shard_map/dot_general | solution.py:52
  147.7 1.9 fusion.5
  149.6 1.0 copy-done.1
  150.6 3.8 %collective-permute-start.8 = (f32[10,1,128]{2,0,1:T(8,128)S(1)}, f32[10,1,128]{2,0,1:T(8,128)S(1)}, u32[]{:S(2)}, u32[]{:S(2)}) collective-permute-start(f32[10,1,128]{2,0,1:T(8,128)S(1)} %get-tuple-element.20), channel_id=1, source_target_pairs={{0,48},{48,96},{96,144},{144,192},{192,240},{240,288},{288,336},{3... | collective-permute-start | bytes 15368 | tf_op jit(solution)/shard_map/ppermute | solution.py:15
  154.5 1.9 collective-permute-start.9
  156.4 0.8 copy.67
  157.2 2.2 collective-permute-done.9
  159.4 1.3 pad_maximum_fusion
  160.7 1.7 fusion.60
  162.4 1.6 copy.59
  164.0 1.7 copy.61
  165.7 1.3 collective-permute-start.11
  167.0 4.4 %collective-permute-start.10 = (f32[10,130,1]{1,2,0:T(1,128)S(1)}, f32[10,130,1]{1,2,0:T(1,128)S(1)}, u32[]{:S(2)}, u32[]{:S(2)}) collective-permute-start(f32[10,130,1]{1,2,0:T(1,128)S(1)} %copy.59), channel_id=1, source_target_pairs={{0,1},{1,2},{2,3},{3,4},{4,5},{5,6},{6,7},{7,8},{8,9},{9,10},{10,1... | collective-permute-start | bytes 15608 | tf_op jit(solution)/shard_map/ppermute | solution.py:15
  172.0 1.6 copy.60
  173.6 1.7 copy.62
  175.3 4.3 %fusion.20 = f32[10,128,128]{2,0,1:T(8,128)S(1)} fusion(f32[10,128,128]{2,0,1:T(8,128)} %copy-done.1, f32[10,130,1]{2,0,1:T(8,128)} %copy.62, f32[10,1,128]{2,0,1:T(8,128)S(1)} %collective-permute-done.9, f32[10,1,128]{2,0,1:T(8,128)S(1)} %collective-permute-done.8, f32[10,130,1]{2,0,1:T(8,128)} %copy.60), kind=kLoop, calls=%fused_computation.37 | loop fusion | flops 2457600 | bytes 1331360 | tf_op jit(solution)/shard_map/add | solution.py:28
  179.6 1.0 copy-done.2
  180.6 3.7 %collective-permute-start.12 = (f32[10,1,128]{2,0,1:T(8,128)S(1)}, f32[10,1,128]{2,0,1:T(8,128)S(1)}, u32[]{:S(2)}, u32[]{:S(2)}) collective-permute-start(f32[10,1,128]{2,0,1:T(8,128)S(1)} %get-tuple-element.18), channel_id=1, source_target_pairs={{0,48},{48,96},{96,144},{144,192},{192,240},{240,288},{288,336},{3... | collective-permute-start | bytes 15368 | tf_op jit(solution)/shard_map/ppermute | solution.py:15
  184.2 1.9 collective-permute-start.13
  186.4 2.8 %collective-permute-done.13 = f32[10,1,128]{2,0,1:T(8,128)S(1)} collective-permute-done((f32[10,1,128]{2,0,1:T(8,128)S(1)}, f32[10,1,128]{2,0,1:T(8,128)S(1)}, u32[]{:S(2)}, u32[]{:S(2)}) %collective-permute-start.13) | collective-permute-done | bytes 5152 | tf_op jit(solution)/shard_map/ppermute | solution.py:18
  189.2 1.3 pad_maximum_fusion.1
  190.5 1.7 fusion.59
  192.2 1.6 copy.63
  193.8 1.7 copy.65
  195.5 1.3 collective-permute-start.15
  196.8 4.5 %collective-permute-start.14 = (f32[10,130,1]{1,2,0:T(1,128)S(1)}, f32[10,130,1]{1,2,0:T(1,128)S(1)}, u32[]{:S(2)}, u32[]{:S(2)}) collective-permute-start(f32[10,130,1]{1,2,0:T(1,128)S(1)} %copy.63), channel_id=1, source_target_pairs={{0,1},{1,2},{2,3},{3,4},{4,5},{5,6},{6,7},{7,8},{8,9},{9,10},{10,1... | collective-permute-start | bytes 15608 | tf_op jit(solution)/shard_map/ppermute | solution.py:15
  202.1 1.6 copy.64
  203.8 1.7 copy.66
  205.4 4.3 %fusion.14 = f32[10,128,128]{2,0,1:T(8,128)S(1)} fusion(f32[10,128,128]{2,0,1:T(8,128)} %copy-done.2, f32[10,130,1]{2,0,1:T(8,128)} %copy.66, f32[10,1,128]{2,0,1:T(8,128)S(1)} %collective-permute-done.13, f32[10,1,128]{2,0,1:T(8,128)S(1)} %collective-permute-done.12, f32[10,130,1]{2,0,1:T(8,128)} %copy.64), kind=kLoop, calls=%fused_computation.23 | loop fusion | flops 2457600 | bytes 1331360 | tf_op jit(solution)/shard_map/add | solution.py:28
  209.7 1.0 copy-done.3
  210.8 0.8 gather_fusion.1
  211.5 0.8 select_select_fusion
  212.3 11.0 %all-to-all-start.2 = ((bf16[48,4,128]{2,1,0:T(4,128)(2,1)}), bf16[48,4,128]{2,1,0:T(4,128)(2,1)S(1)}, u32[]{:S(2)}, u32[]{:S(2)}) async-start(bf16[48,4,128]{2,1,0:T(4,128)(2,1)} %select_select_fusion), calls=%async_computation.2 | async-start | bytes 98304 | tf_op jit(solution)/shard_map/all_to_all | solution.py:119
  223.4 2.3 copy.72
  225.7 9.8 %all-to-all-done.2 = bf16[48,4,128]{2,1,0:T(4,128)(2,1)S(1)} async-done(((bf16[48,4,128]{2,1,0:T(4,128)(2,1)}), bf16[48,4,128]{2,1,0:T(4,128)(2,1)S(1)}, u32[]{:S(2)}, u32[]{:S(2)}) %all-to-all-start.2) | async-done | bytes 49184 | tf_op jit(solution)/shard_map/all_to_all | solution.py:119
  236.3 1.7 fusion
  238.0 0.8 fusion.52
  (60 shorter events, 6.2 us)
Async XLA Ops:
  0.6 70.0 %copy-start = (bf16[1,96,128,128]{3,2,1,0:T(8,128)(2,1)S(1)}, bf16[1,96,128,128]{3,2,1,0:T(8,128)(2,1)}, u32[]{:S(2)}) copy-start(bf16[1,96,128,128]{3,2,1,0:T(8,128)(2,1)} %param.12) | copy-start | bytes 9437188
  0.6 43.8 %copy-start.5 = (f32[8,64,128]{2,1,0:T(8,128)S(1)}, f32[8,64,128]{2,1,0:T(8,128)}, u32[]{:S(2)}) copy-start(f32[8,64,128]{2,1,0:T(8,128)} %param.8) | copy-start | bytes 786436
  0.7 35.1 %copy-start.9 = (s32[1,96]{1,0:T(1,128)S(1)}, s32[1,96]{1,0:T(1,128)}, u32[]{:S(2)}) copy-start(s32[1,96]{1,0:T(1,128)} %param.13) | copy-start | bytes 1156
  1.6 28.8 %collective-permute-start = (f32[8,1,128]{2,1,0:T(1,128)S(1)}, f32[8,1,128]{2,1,0:T(1,128)S(1)}, u32[]{:S(2)}, u32[]{:S(2)}) collective-permute-start(f32[8,1,128]{2,1,0:T(1,128)S(1)} %get-tuple-element.28), channel_id=1, source_target_pairs={{0,48},{48,96},{96,144},{144,192},{192,240},{240,288},{288,336},{3... | collective-permute-start | bytes 12296 | tf_op jit(solution)/shard_map/ppermute | solution.py:15
  6.3 24.0 %collective-permute-start.1 = (f32[8,1,128]{2,1,0:T(1,128)S(1)}, f32[8,1,128]{2,1,0:T(1,128)S(1)}, u32[]{:S(2)}, u32[]{:S(2)}) collective-permute-start(f32[8,1,128]{2,1,0:T(1,128)S(1)} %get-tuple-element.29), channel_id=1, source_target_pairs={{48,0},{96,48},{144,96},{192,144},{240,192},{288,240},{336,288},{3... | collective-permute-start | bytes 12296 | tf_op jit(solution)/shard_map/ppermute | solution.py:18
  19.4 55.7 %all-to-all-start = ((s32[48,4,1]{1,2,0:T(1,128)}), s32[48,4,1]{1,2,0:T(1,128)}, u32[]{:S(2)}, u32[]{:S(2)}) async-start(s32[48,4,1]{1,2,0:T(1,128)} %bitcast.2), calls=%async_computation | async-start | bytes 49152 | tf_op jit(solution)/shard_map/all_to_all | solution.py:109
  31.5 8.9 %collective-permute-start.2 = (f32[8,66,1]{2,1,0:T(8,128)S(1)}, f32[8,66,1]{2,1,0:T(8,128)S(1)}, u32[]{:S(2)}, u32[]{:S(2)}) collective-permute-start(f32[8,66,1]{2,1,0:T(8,128)S(1)} %get-tuple-element.24), channel_id=1, source_target_pairs={{0,1},{1,2},{2,3},{3,4},{4,5},{5,6},{6,7},{7,8},{8,9},{9,10},{10,1... | collective-permute-start | bytes 6344 | tf_op jit(solution)/shard_map/ppermute | solution.py:15
  34.5 9.9 %collective-permute-start.3 = (f32[8,66,1]{2,1,0:T(8,128)S(1)}, f32[8,66,1]{2,1,0:T(8,128)S(1)}, u32[]{:S(2)}, u32[]{:S(2)}) collective-permute-start(f32[8,66,1]{2,1,0:T(8,128)S(1)} %get-tuple-element.25), channel_id=1, source_target_pairs={{1,0},{2,1},{3,2},{4,3},{5,4},{6,5},{7,6},{8,7},{9,8},{10,9},{11,1... | collective-permute-start | bytes 6344 | tf_op jit(solution)/shard_map/ppermute | solution.py:18
  44.8 6.4 %collective-permute-start.4 = (f32[8,1,128]{2,1,0:T(1,128)S(1)}, f32[8,1,128]{2,1,0:T(1,128)S(1)}, u32[]{:S(2)}, u32[]{:S(2)}) collective-permute-start(f32[8,1,128]{2,1,0:T(1,128)S(1)} %get-tuple-element.26), channel_id=1, source_target_pairs={{0,48},{48,96},{96,144},{144,192},{192,240},{240,288},{288,336},{3... | collective-permute-start | bytes 12296 | tf_op jit(solution)/shard_map/ppermute | solution.py:15
  49.2 4.9 %collective-permute-start.5 = (f32[8,1,128]{2,1,0:T(1,128)S(1)}, f32[8,1,128]{2,1,0:T(1,128)S(1)}, u32[]{:S(2)}, u32[]{:S(2)}) collective-permute-start(f32[8,1,128]{2,1,0:T(1,128)S(1)} %get-tuple-element.27), channel_id=1, source_target_pairs={{48,0},{96,48},{144,96},{192,144},{240,192},{288,240},{336,288},{3... | collective-permute-start | bytes 12296 | tf_op jit(solution)/shard_map/ppermute | solution.py:18
  54.2 13.5 %copy-start.8 = (f32[12,8]{0,1:T(8,128)S(1)}, f32[12,8]{0,1:T(8,128)}, u32[]{:S(2)}) copy-start(f32[12,8]{0,1:T(8,128)} %param.10) | copy-start | bytes 1156
  54.4 8.5 %collective-permute-start.6 = (f32[8,66,1]{2,1,0:T(8,128)S(1)}, f32[8,66,1]{2,1,0:T(8,128)S(1)}, u32[]{:S(2)}, u32[]{:S(2)}) collective-permute-start(f32[8,66,1]{2,1,0:T(8,128)S(1)} %get-tuple-element.22), channel_id=1, source_target_pairs={{0,1},{1,2},{2,3},{3,4},{4,5},{5,6},{6,7},{7,8},{8,9},{9,10},{10,1... | collective-permute-start | bytes 6344 | tf_op jit(solution)/shard_map/ppermute | solution.py:15
  57.5 9.9 %collective-permute-start.7 = (f32[8,66,1]{2,1,0:T(8,128)S(1)}, f32[8,66,1]{2,1,0:T(8,128)S(1)}, u32[]{:S(2)}, u32[]{:S(2)}) collective-permute-start(f32[8,66,1]{2,1,0:T(8,128)S(1)} %get-tuple-element.23), channel_id=1, source_target_pairs={{1,0},{2,1},{3,2},{4,3},{5,4},{6,5},{7,6},{8,7},{9,8},{10,9},{11,1... | collective-permute-start | bytes 6344 | tf_op jit(solution)/shard_map/ppermute | solution.py:18
  75.0 70.2 %all-to-all-start.1 = ((f32[192,12,128]{2,1,0:T(8,128)}), f32[192,12,128]{2,1,0:T(8,128)}, u32[]{:S(2)}, u32[]{:S(2)}) async-start(f32[192,12,128]{2,1,0:T(8,128)} %copy.55), calls=%async_computation.1 | async-start | bytes 3145728 | tf_op jit(solution)/shard_map/all_to_all | solution.py:108
  86.8 60.8 %copy-start.6 = (f32[10,12]{1,0:T(8,128)S(1)}, f32[10,12]{1,0:T(8,128)}, u32[]{:S(2)}) copy-start(f32[10,12]{1,0:T(8,128)} %param.11) | copy-start | bytes 1444
  145.2 2.4 %copy-start.4 = (f32[10,128,128]{2,1,0:T(8,128)S(1)}, f32[10,128,128]{2,1,0:T(8,128)}, u32[]{:S(2)}) copy-start(f32[10,128,128]{2,1,0:T(8,128)} %param.9) | copy-start | bytes 1966084
  149.6 1.0 copy-start.1
  150.6 6.6 %collective-permute-start.8 = (f32[10,1,128]{2,0,1:T(8,128)S(1)}, f32[10,1,128]{2,0,1:T(8,128)S(1)}, u32[]{:S(2)}, u32[]{:S(2)}) collective-permute-start(f32[10,1,128]{2,0,1:T(8,128)S(1)} %get-tuple-element.20), channel_id=1, source_target_pairs={{0,48},{48,96},{96,144},{144,192},{192,240},{240,288},{288,336},{3... | collective-permute-start | bytes 15368 | tf_op jit(solution)/shard_map/ppermute | solution.py:15
  154.5 5.0 %collective-permute-start.9 = (f32[10,1,128]{2,0,1:T(8,128)S(1)}, f32[10,1,128]{2,0,1:T(8,128)S(1)}, u32[]{:S(2)}, u32[]{:S(2)}) collective-permute-start(f32[10,1,128]{2,0,1:T(8,128)S(1)} %get-tuple-element.21), channel_id=1, source_target_pairs={{48,0},{96,48},{144,96},{192,144},{240,192},{288,240},{336,288},{3... | collective-permute-start | bytes 15368 | tf_op jit(solution)/shard_map/ppermute | solution.py:18
  165.7 7.9 %collective-permute-start.11 = (f32[10,130,1]{1,2,0:T(1,128)S(1)}, f32[10,130,1]{1,2,0:T(1,128)S(1)}, u32[]{:S(2)}, u32[]{:S(2)}) collective-permute-start(f32[10,130,1]{1,2,0:T(1,128)S(1)} %copy.61), channel_id=1, source_target_pairs={{1,0},{2,1},{3,2},{4,3},{5,4},{6,5},{7,6},{8,7},{9,8},{10,9},{11,1... | collective-permute-start | bytes 15608 | tf_op jit(solution)/shard_map/ppermute | solution.py:18
  167.0 5.0 %collective-permute-start.10 = (f32[10,130,1]{1,2,0:T(1,128)S(1)}, f32[10,130,1]{1,2,0:T(1,128)S(1)}, u32[]{:S(2)}, u32[]{:S(2)}) collective-permute-start(f32[10,130,1]{1,2,0:T(1,128)S(1)} %copy.59), channel_id=1, source_target_pairs={{0,1},{1,2},{2,3},{3,4},{4,5},{5,6},{6,7},{7,8},{8,9},{9,10},{10,1... | collective-permute-start | bytes 15608 | tf_op jit(solution)/shard_map/ppermute | solution.py:15
  179.6 1.0 copy-start.2
  180.6 5.8 %collective-permute-start.12 = (f32[10,1,128]{2,0,1:T(8,128)S(1)}, f32[10,1,128]{2,0,1:T(8,128)S(1)}, u32[]{:S(2)}, u32[]{:S(2)}) collective-permute-start(f32[10,1,128]{2,0,1:T(8,128)S(1)} %get-tuple-element.18), channel_id=1, source_target_pairs={{0,48},{48,96},{96,144},{144,192},{192,240},{240,288},{288,336},{3... | collective-permute-start | bytes 15368 | tf_op jit(solution)/shard_map/ppermute | solution.py:15
  184.2 5.0 %collective-permute-start.13 = (f32[10,1,128]{2,0,1:T(8,128)S(1)}, f32[10,1,128]{2,0,1:T(8,128)S(1)}, u32[]{:S(2)}, u32[]{:S(2)}) collective-permute-start(f32[10,1,128]{2,0,1:T(8,128)S(1)} %get-tuple-element.19), channel_id=1, source_target_pairs={{48,0},{96,48},{144,96},{192,144},{240,192},{288,240},{336,288},{3... | collective-permute-start | bytes 15368 | tf_op jit(solution)/shard_map/ppermute | solution.py:18
  195.5 8.3 %collective-permute-start.15 = (f32[10,130,1]{1,2,0:T(1,128)S(1)}, f32[10,130,1]{1,2,0:T(1,128)S(1)}, u32[]{:S(2)}, u32[]{:S(2)}) collective-permute-start(f32[10,130,1]{1,2,0:T(1,128)S(1)} %copy.65), channel_id=1, source_target_pairs={{1,0},{2,1},{3,2},{4,3},{5,4},{6,5},{7,6},{8,7},{9,8},{10,9},{11,1... | collective-permute-start | bytes 15608 | tf_op jit(solution)/shard_map/ppermute | solution.py:18
  196.8 5.3 %collective-permute-start.14 = (f32[10,130,1]{1,2,0:T(1,128)S(1)}, f32[10,130,1]{1,2,0:T(1,128)S(1)}, u32[]{:S(2)}, u32[]{:S(2)}) collective-permute-start(f32[10,130,1]{1,2,0:T(1,128)S(1)} %copy.63), channel_id=1, source_target_pairs={{0,1},{1,2},{2,3},{3,4},{4,5},{5,6},{6,7},{7,8},{8,9},{9,10},{10,1... | collective-permute-start | bytes 15608 | tf_op jit(solution)/shard_map/ppermute | solution.py:15
  205.4 17.9 %copy-start.7 = (s32[1,96,1]{1,2,0:T(1,128)S(1)}, s32[1,96,1]{1,2,0:T(1,128)}, u32[]{:S(2)}) copy-start(s32[1,96,1]{1,2,0:T(1,128)} %param.15) | copy-start | bytes 1156
  209.7 1.0 copy-start.3
  212.3 23.2 %all-to-all-start.2 = ((bf16[48,4,128]{2,1,0:T(4,128)(2,1)}), bf16[48,4,128]{2,1,0:T(4,128)(2,1)S(1)}, u32[]{:S(2)}, u32[]{:S(2)}) async-start(bf16[48,4,128]{2,1,0:T(4,128)(2,1)} %select_select_fusion), calls=%async_computation.2 | async-start | bytes 98304 | tf_op jit(solution)/shard_map/all_to_all | solution.py:119
  236.3 1.7 copy-start.10
where the time goes:
time: 241 us; the launch traced here: 239 us
  waiting for transfers between devices  91.9 us (38%)
  starting transfers between devices  85.6 us (36%)
  local copies, waits for them, and re-layouts  30.6 us (13%)
  other arithmetic  18.9 us (8%)
  matrix products  10.7 us (4%)
    all_to_all x1, waiting for transfers between devices, body(): lax.all_to_all(send_values, 'gy', split_axis=0, concat_axis=0, tiled=True)  56.3 us
    ppermute x8, starting transfers between devices, with_halo(): lax.ppermute(lax.slice_in_dim(block, block.shape[dim] - width, None, axis...  31.7 us
    ppermute x8, starting transfers between devices, with_halo(): lax.ppermute(lax.slice_in_dim(block, 0, width, axis=dim), axis, backward)  20.1 us
    ppermute x8, waiting for transfers between devices, with_halo(): lax.ppermute(lax.slice_in_dim(block, 0, width, axis=dim), axis, backward)  16.5 us
    all_to_all x1, starting transfers between devices, body(): lax.all_to_all(send_values, 'gy', split_axis=0, concat_axis=0, tiled=True)  11.8 us
    all_to_all x1, starting transfers between devices, body(): lax.all_to_all(send_back, 'gy', split_axis=0, concat_axis=0, tiled=True)  11 us
    all_to_all x1, starting transfers between devices, body(): lax.all_to_all(send_ids, 'gy', split_axis=0, concat_axis=0, tiled=True)  11 us
    all_to_all x1, waiting for transfers between devices, body(): lax.all_to_all(send_back, 'gy', split_axis=0, concat_axis=0, tiled=True)  9.83 us
  transfers between devices with their start and end apart: 19, of which 11 were waited for; matrix products, arithmetic and copies ran while one was open for 9% of the time, Pallas kernels for 0%

commit v1 on v0

v1 whole, which is shorter than its diff:
```python
import functools

import jax
import jax.numpy as jnp
from jax import lax
from jax.experimental import pallas as pl
from jax.experimental.pallas import tpu as pltpu
from jax.sharding import PartitionSpec as P

MESH = pl.DeviceIdType.MESH
RATE = 0.2
CAP = 4
F32, BF16, I32 = jnp.float32, jnp.bfloat16, jnp.int32
LANES = 128
NT = (((1,), (1,)), ((), ()))
CHUNK = 16


def iota(shape, dim):
    return lax.broadcasted_iota(I32, shape, dim)


def pack_sides(levels, rows):
    pair = lax.shift_right_logical(iota((rows, LANES), 1), 1)
    packed = jnp.zeros((rows, LANES), F32)
    for n, field in enumerate(levels):
        packed = jnp.where(pair == n, pltpu.roll(field, 2 * n, 1) if n else field, packed)
        packed = jnp.where(pair == 32 + n, pltpu.roll(field, 66 + 2 * n, 1), packed)
    return packed


class Halo:
    def __init__(self, place, refs, rows, count):
        self.gx, self.gy, self.ngx, self.ngy = place
        (self.top, self.bot, self.cl, self.cr, self.dg, self.ptl, self.ptr, self.pe, self.pk, self.ss, self.rs) = refs
        self.rows, self.count = rows, count

    def start(self, field, packed):
        rows = self.rows
        tall = packed
        if rows < LANES:
            tall = jnp.concatenate([packed, jnp.zeros((LANES - rows, LANES), F32)], axis=0)
        turned = tall.T
        cs = self.ptl.shape[0]
        self.ptl[...] = turned[0:cs]
        self.ptr[...] = turned[64 : 64 + cs]
        self.pe[0] = packed[0:8]
        self.pe[1] = packed[rows - 8 : rows]
        self.pk[...] = packed
        up, down = lax.rem(self.gx + self.ngx - 1, self.ngx), lax.rem(self.gx + 1, self.ngx)
        left, right = lax.rem(self.gy + self.ngy - 1, self.ngy), lax.rem(self.gy + 1, self.ngy)
        plan = (
            (field.at[:, 0:8], self.bot, (up, self.gy)),
            (field.at[:, rows - 8 : rows], self.top, (down, self.gy)),
            (self.ptl, self.cr, (self.gx, left)),
            (self.ptr, self.cl, (self.gx, right)),
            (self.pe.at[0], self.dg.at[3], (up, left)),
            (self.pe.at[0], self.dg.at[2], (up, right)),
            (self.pe.at[1], self.dg.at[1], (down, left)),
            (self.pe.at[1], self.dg.at[0], (down, right)),
        )
        self.copies = [
            pltpu.make_async_remote_copy(
                src_ref=src,
                dst_ref=dst,
                send_sem=self.ss.at[n],
                recv_sem=self.rs.at[n],
                device_id=device,
                device_id_type=MESH,
            )
            for n, (src, dst, device) in enumerate(plan)
        ]
        for copy in self.copies:
            copy.start()

    def arrive(self):
        for copy in self.copies:
            copy.wait_recv()
        rows = self.rows
        lane = iota((1, LANES), 1)
        low = lane < 64
        self.has_top, self.has_bot = self.gx > 0, self.gx < self.ngx - 1
        edge = jnp.where(low, jnp.where(self.gy > 0, 1, 0), jnp.where(self.gy < self.ngy - 1, 1, 0)) > 0
        cs = self.cl.shape[0]
        fill = jnp.zeros((64 - cs, LANES), F32)
        turned = jnp.concatenate([self.cl[...], fill, self.cr[...], fill], axis=0)
        sides = turned.T[0:rows]
        above = jnp.where(low, pltpu.roll(self.dg[0], 64, 1), pltpu.roll(self.dg[1], 64, 1))
        below = jnp.where(low, pltpu.roll(self.dg[2], 64, 1), pltpu.roll(self.dg[3], 64, 1))
        above = jnp.where(self.has_top, above, 0.0)
        below = jnp.where(self.has_bot, below, 0.0)
        rim = jnp.where(edge, jnp.concatenate([above, sides, below], axis=0), 0.0)
        total = rows + 16
        up = pltpu.roll(rim, 1, 0)[8 : rows + 8]
        down = pltpu.roll(rim, total - 1, 0)[8 : rows + 8]
        near = sides + self.pk[...]
        beside = jnp.where(low, pltpu.roll(near, 1, 1), pltpu.roll(near, LANES - 1, 1))
        mid = sides + RATE * (up + down + beside - 4.0 * sides)
        self.rim, self.mid = rim, jnp.where(edge, mid, 0.0)

    def two_steps(self, n, field, rim_ref, mid_ref):
        rows = self.rows
        total = rows + 16
        rim, rim_mid = rim_ref[...], mid_ref[...]
        top = jnp.where(self.has_top, self.top[n], 0.0)
        bot = jnp.where(self.has_bot, self.bot[n], 0.0)
        whole = jnp.concatenate([top, field, bot], axis=0)
        lane, row = iota((total, LANES), 1), iota((total, LANES), 0)
        to_first, to_last = LANES - 1 - 2 * n, 63 - 2 * n
        beside = (
            jnp.where(lane == 0, pltpu.roll(rim, to_first, 1), pltpu.roll(whole, 1, 1))
            + jnp.where(lane == LANES - 1, pltpu.roll(rim, to_last, 1), pltpu.roll(whole, LANES - 1, 1))
            + pltpu.roll(whole, 1, 0)
            + pltpu.roll(whole, total - 1, 0)
        )
        mid = whole + RATE * (beside - 4.0 * whole)
        first_row, last_row = jnp.where(self.has_top, 0, 8), jnp.where(self.has_bot, total, rows + 8)
        mid = jnp.where((row >= first_row) & (row < last_row), mid, 0.0)
        own = mid[8 : rows + 8]
        lane = iota((rows, LANES), 1)
        beside = (
            jnp.where(lane == 0, pltpu.roll(rim_mid, to_first, 1), pltpu.roll(own, 1, 1))
            + jnp.where(lane == LANES - 1, pltpu.roll(rim_mid, to_last, 1), pltpu.roll(own, LANES - 1, 1))
            + pltpu.roll(mid, 1, 0)[8 : rows + 8]
            + pltpu.roll(mid, total - 1, 0)[8 : rows + 8]
        )
        return own + RATE * (beside - 4.0 * own)

    def wait_sent(self):
        for copy in self.copies:
            copy.wait_send()


def kernel(
    sizes,
    atm_ref,
    ocean_hbm,
    coef_ref,
    mix_ref,
    share_hbm,
    src_ref,
    dest_ref,
    owner_ref,
    final_hbm,
    aerial_ref,
    share,
    ocean,
    final,
    surf,
    mixed,
    lists,
    table,
    table_s,
    id_send,
    id_recv,
    f_send,
    f_recv,
    hits,
    spread,
    pick,
    s_send,
    s_recv,
    rims,
    mids,
    share_sem,
    ocean_sem,
    table_sem,
    final_sem,
    id_ss,
    id_rs,
    f_ss,
    f_rs,
    s_ss,
    s_rs,
    *halo_refs,
):
    ngx, nx, nz = sizes
    ngy = nx * nz
    slots = ngy * CAP
    chunks = ngy // CHUNK
    la, ra = atm_ref.shape[0], atm_ref.shape[1]
    lo, ro = ocean.shape[0], ocean.shape[1]
    nb = src_ref.shape[1]
    fluxes = coef_ref.shape[0]
    gx, gy = lax.axis_index("gx"), lax.axis_index("gy")
    my_x, my_z = lax.div(gy, nz), lax.rem(gy, nz)
    place = (gx, gy, ngx, ngy)

    share_copy = pltpu.make_async_copy(share_hbm.at[0], share, share_sem)
    share_copy.start()
    ocean_copy = pltpu.make_async_copy(ocean_hbm, ocean, ocean_sem)
    ocean_copy.start()

    def shift(i):
        k = lax.div(i, nx)
        dx = lax.rem(i, nx)
        dz = lax.div(k + 1, 2) * (2 * lax.rem(k, 2) - 1)
        return dx, dz

    def ahead(i):
        dx, dz = shift(i)
        return lax.rem(my_x + dx, nx) * nz + lax.rem(my_z + dz + nz, nz)

    def behind(i):
        dx, dz = shift(i)
        return lax.rem(my_x - dx + nx, nx) * nz + lax.rem(my_z - dz + nz, nz)

    barrier = pltpu.get_barrier_semaphore()
    up, down = lax.rem(gx + ngx - 1, ngx), lax.rem(gx + 1, ngx)
    left, right = lax.rem(gy + ngy - 1, ngy), lax.rem(gy + 1, ngy)
    for device in ((up, gy), (down, gy), (up, left), (up, right), (down, left), (down, right)):
        pl.semaphore_signal(barrier, inc=1, device_id=device, device_id_type=MESH)

    def greet(i, carry):
        pl.semaphore_signal(barrier, inc=1, device_id=(gx, ahead(i)), device_id_type=MESH)
        return carry

    lax.fori_loop(1, ngy, greet, 0)

    atm_halo = Halo(place, halo_refs[0:11], ra, la)
    top_halo = Halo(place, halo_refs[11:22], ro, 1)
    low_halo = Halo(place, halo_refs[22:33], ro, lo - 1)

    lists[...] = jnp.full((8, LANES), -1, I32)
    lists[0:1, 0:nb] = owner_ref[...]
    lists[1:2, 0:nb] = dest_ref[...]
    own_row, dest_row = lists[0:1, :], lists[1:2, :]
    lane = iota((1, LANES), 1)
    own_x = jnp.zeros((1, LANES), I32)
    for t in range(1, nx):
        own_x = own_x + jnp.where(own_row >= t * nz, 1, 0)
    own_z = own_row - own_x * nz
    dx = own_x - my_x
    dx = jnp.where(dx < 0, dx + nx, dx)
    dz = own_z - my_z
    dz = jnp.where(dz < 0, dz + nz, dz)
    k = jnp.where(dz == 0, 0, jnp.where(dz <= nz // 2, 2 * dz - 1, 2 * (nz - dz)))
    step_row = k * nx + dx
    sq = (LANES, LANES)
    sub_q, lane_q = iota(sq, 0), iota(sq, 1)
    own_sq = jnp.broadcast_to(own_row, sq)
    same = (own_sq == own_sq.T) & (sub_q < lane_q)
    rank = jnp.sum(jnp.where(same, 1, 0), axis=0, keepdims=True)
    slot_row = jnp.where(lane < nb, step_row * CAP + rank, -1)
    slot_col = jnp.broadcast_to(slot_row, sq).T
    table[...] = jnp.zeros((8, LANES), I32)
    table[0:1, :] = jnp.clip(slot_row, 0, slots - 1)
    for b in range(-(-slots // LANES)):
        hit = slot_col == lane_q + b * LANES
        block = jnp.sum(jnp.where(hit, sub_q, 0), axis=0, keepdims=True)
        table[1 + b : 2 + b, :] = jnp.clip(block, 0, nb - 1)
    table_copy = pltpu.make_async_copy(table, table_s, table_sem)
    table_copy.start()
    wide = (ngy, LANES)
    step_i, lane_i = iota(wide, 0), iota(wide, 1)
    slot_w = jnp.broadcast_to(slot_row, wide)
    line_w = jnp.broadcast_to((dest_row + 1).astype(F32), wide)
    ids = jnp.zeros(wide, F32)
    for j in range(CAP):
        line = jnp.sum(jnp.where(slot_w == step_i * CAP + j, line_w, 0.0), axis=1, keepdims=True)
        ids = jnp.where(lax.rem(lane_i, CAP) == j, jnp.broadcast_to(line, wide), ids)
    ids = jnp.where(lax.div(lane_i, 16) == lax.rem(step_i, 8), ids, 0.0)
    id_send[...] = ids.reshape(ngy, 1, LANES)
    id_recv[0] = id_send[0]

    atm_packed = pack_sides([atm_ref[l] for l in range(la)], ra)

    pl.semaphore_wait(barrier, ngy - 1 + 6)

    atm_halo.start(atm_ref, atm_packed)

    def id_copy(i):
        return pltpu.make_async_remote_copy(
            src_ref=id_send.at[i],
            dst_ref=id_recv.at[i],
            send_sem=id_ss,
            recv_sem=id_rs,
            device_id=(gx, ahead(i)),
            device_id_type=MESH,
        )

    def send_ids(i, carry):
        id_copy(i).start()
        return carry

    lax.fori_loop(1, ngy, send_ids, 0)

    atm_halo.arrive()
    rims[0, 0 : ra + 16] = atm_halo.rim
    mids[0, 0:ra] = atm_halo.mid

    def atm_level(l, carry):
        surf[l] = atm_halo.two_steps(l, atm_ref[l], rims.at[0, 0 : ra + 16], mids.at[0, 0:ra])
        return carry

    lax.fori_loop(0, la, atm_level, 0)

    band = 16

    def flux_band(c, carry):
        r0 = pl.multiple_of(c * band, band)
        fields = [surf[l, pl.ds(r0, band)] for l in range(la)]
        flux = []
        for kk in range(fluxes):
            total = coef_ref[kk, 0] * fields[0]
            for l in range(1, la):
                total = total + coef_ref[kk, l] * fields[l]
            flux.append(jnp.tanh(total).astype(BF16).astype(F32))
        for l in range(lo):
            total = mix_ref[l, 0] * flux[0]
            for kk in range(1, fluxes):
                total = total + mix_ref[l, kk] * flux[kk]
            total = 0.5 * total
            for j in range(CAP):
                mixed[pl.ds(pl.multiple_of((l * CAP + j) * ra + r0, band), band)] = total
        return carry

    lax.fori_loop(0, ra // band, flux_band, 0)

    share_copy.wait()
    table_copy.wait()

    f_rows = f_send.shape[1]
    used = lo * CAP
    slot_of_row = lax.rem(iota((used, LANES), 0), CAP)

    def f_copy(i):
        return pltpu.make_async_remote_copy(
            src_ref=f_send.at[i],
            dst_ref=f_recv.at[i],
            send_sem=f_ss,
            recv_sem=f_rs.at[lax.div(i, CHUNK)],
            device_id=(gx, ahead(i)),
            device_id_type=MESH,
        )

    def contribution(i):
        left_parts, right_parts = [], []
        for j in range(CAP):
            s = i * CAP + j
            q = jnp.clip(table_s[1 + lax.div(s, LANES), lax.rem(s, LANES)], 0, nb - 1)
            rows = mixed[pl.ds(src_ref[0, q], used, stride=ra), :]
            rows = jnp.where(slot_of_row == j, rows, 0.0)
            rows = jnp.concatenate([rows, jnp.zeros((f_rows - used, LANES), F32)], axis=0)
            left_parts.append(rows.astype(BF16))
            right_parts.append(share[q])
        return jnp.dot(
            jnp.concatenate(left_parts, axis=1),
            jnp.concatenate(right_parts, axis=0),
            preferred_element_type=F32,
        ).astype(BF16)

    def send_blocks(t, carry):
        i = ngy - 1 - t
        f_send[i] = contribution(i)
        f_copy(i).start()
        return carry

    lax.fori_loop(0, ngy - 1, send_blocks, 0)
    f_recv[0] = contribution(0)

    pltpu.make_async_remote_copy(
        src_ref=id_send.at[1:ngy],
        dst_ref=id_recv.at[1:ngy],
        send_sem=id_ss,
        recv_sem=id_rs,
        device_id=(gx, gy),
        device_id_type=MESH,
    ).wait_recv()
    line_of_row = iota((ro, LANES), 0) + 1
    level_of_lane = lax.rem(lax.div(iota((ro, LANES), 1), CAP), CAP)
    for g in range(ngy // 8):
        ids_row = id_recv[8 * g]
        for t in range(1, 8):
            ids_row = ids_row + id_recv[8 * g + t]
        hit = jnp.where(jnp.broadcast_to(ids_row.astype(I32), (ro, LANES)) == line_of_row, 1.0, 0.0)
        hits[:, g * LANES : (g + 1) * LANES] = hit.astype(BF16)
        half = (g % 2) * LANES
        for l in range(CAP):
            spread[g // 2, l * ro : (l + 1) * ro, half : half + LANES] = jnp.where(
                level_of_lane == l, hit, 0.0
            ).astype(BF16)
    chosen = iota((slots, ngy * 16), 0)
    chosen = jnp.where(
        iota((slots, ngy * 16), 1) == lax.div(chosen, CAP) * 16 + lax.rem(chosen, CAP), 1.0, 0.0
    ).astype(BF16)
    pick[...] = lax.dot_general(chosen, hits[...], NT, preferred_element_type=F32).astype(BF16)

    ocean_copy.wait()

    def land(c, l0, l1):
        base = 4 * (l0 // 4)
        rows = f_recv[c * CHUNK : (c + 1) * CHUNK, base * CAP : base * CAP + 16, :]
        landed = jnp.dot(
            spread[c, (l0 - base) * ro : (l1 - base) * ro, :],
            rows.reshape(CHUNK * 16, LANES),
            preferred_element_type=F32,
        )
        for l in range(l0, l1):
            ocean[l] = ocean[l] + landed[(l - l0) * ro : (l - l0 + 1) * ro]

    for c in reversed(range(chunks)):
        first = 1 if c == 0 else c * CHUNK
        here = pl.ds(first, (c + 1) * CHUNK - first)
        pltpu.make_async_remote_copy(
            src_ref=f_send.at[here],
            dst_ref=f_recv.at[here],
            send_sem=f_ss,
            recv_sem=f_rs.at[c],
            device_id=(gx, gy),
            device_id_type=MESH,
        ).wait_recv()
        if c:
            for l0 in range(0, lo, 4):
                land(c, l0, min(lo, l0 + 4))
    land(0, 0, 1)
    top_halo.start(ocean.at[0:1], pack_sides([ocean[0]], ro))
    land(0, 1, 4)
    for l0 in range(4, lo, 4):
        land(0, l0, min(lo, l0 + 4))
    low_halo.start(ocean.at[1:lo], pack_sides([ocean[l] for l in range(1, lo)], ro))

    top_halo.arrive()
    rims[1] = top_halo.rim
    mids[1] = top_halo.mid
    skin = top_halo.two_steps(0, ocean[0], rims.at[1], mids.at[1])
    final[0] = skin
    lines = jnp.dot(pick[...], skin.astype(BF16), preferred_element_type=F32)
    s_send[...] = lines.reshape(slots, 1, LANES)
    s_recv[0:CAP] = s_send[0:CAP]

    def s_copy(i):
        here = pl.ds(i * CAP, CAP)
        return pltpu.make_async_remote_copy(
            src_ref=s_send.at[here],
            dst_ref=s_recv.at[here],
            send_sem=s_ss,
            recv_sem=s_rs,
            device_id=(gx, behind(i)),
            device_id_type=MESH,
        )

    def send_lines(t, carry):
        s_copy(ngy - 1 - t).start()
        return carry

    lax.fori_loop(0, ngy - 1, send_lines, 0)

    low_halo.arrive()
    rims[2] = low_halo.rim
    mids[2] = low_halo.mid

    def low_level(n, carry):
        final[n + 1] = low_halo.two_steps(n, ocean[n + 1], rims.at[2], mids.at[2])
        return carry

    lax.fori_loop(0, lo - 1, low_level, 0)
    final_copy = pltpu.make_async_copy(final, final_hbm, final_sem)
    final_copy.start()

    rest = pl.ds(CAP, slots - CAP)
    pltpu.make_async_remote_copy(
        src_ref=s_send.at[rest],
        dst_ref=s_recv.at[rest],
        send_sem=s_ss,
        recv_sem=s_rs,
        device_id=(gx, gy),
        device_id_type=MESH,
    ).wait_recv()
    row_a = iota((ra, LANES), 0)

    def home(b, total):
        left_parts, right_parts = [], []
        for j in range(4):
            q = b * 4 + j
            line = jnp.broadcast_to(s_recv[jnp.clip(table_s[0, q], 0, slots - 1)], (ra, LANES))
            left_parts.append(jnp.where(row_a == src_ref[0, q], line, 0.0).astype(BF16))
            right_parts.append(share[q])
        return total + lax.dot_general(
            jnp.concatenate(left_parts, axis=1),
            jnp.concatenate(right_parts, axis=1),
            NT,
            preferred_element_type=F32,
        )

    aerial_ref[...] = lax.fori_loop(0, nb // 4, home, jnp.zeros((ra, LANES), F32))

    for halo in (atm_halo, top_halo, low_halo):
        halo.wait_sent()
    for buffer, sem, first in ((id_send, id_ss, 1), (f_send, f_ss, 1), (s_send, s_ss, CAP)):
        here = pl.ds(first, buffer.shape[0] - first)
        pltpu.make_async_remote_copy(
            src_ref=buffer.at[here],
            dst_ref=buffer.at[here],
            send_sem=sem,
            recv_sem=s_rs,
            device_id=(gx, gy),
            device_id_type=MESH,
        ).wait_send()
    final_copy.wait()


def halo_scratch(rows, count):
    cs = -(-2 * count // 8) * 8
    return [
        pltpu.VMEM((count, 8, LANES), F32),
        pltpu.VMEM((count, 8, LANES), F32),
        pltpu.VMEM((cs, LANES), F32),
        pltpu.VMEM((cs, LANES), F32),
        pltpu.VMEM((4, 8, LANES), F32),
        pltpu.VMEM((cs, LANES), F32),
        pltpu.VMEM((cs, LANES), F32),
        pltpu.VMEM((2, 8, LANES), F32),
        pltpu.VMEM((rows, LANES), F32),
        pltpu.SemaphoreType.DMA((8,)),
        pltpu.SemaphoreType.DMA((8,)),
    ]


def body(sizes, atm_state, ocean_temp, flux_coef, flux_mix, share, src, dest, owner):
    ngx, nx, nz = sizes
    ngy = nx * nz
    slots = ngy * CAP
    la, ra, _ = atm_state.shape
    lo, ro, _ = ocean_temp.shape
    nb = src.shape[1]
    f_rows = -(-lo * CAP // 16) * 16
    vmem = pl.BlockSpec(memory_space=pltpu.VMEM)
    smem = pl.BlockSpec(memory_space=pltpu.SMEM)
    anywhere = pl.BlockSpec(memory_space=pl.ANY)
    dma = pltpu.SemaphoreType.DMA
    return pl.pallas_call(
        functools.partial(kernel, sizes),
        out_shape=(
            jax.ShapeDtypeStruct(ocean_temp.shape, F32),
            jax.ShapeDtypeStruct((ra, LANES), F32),
        ),
        in_specs=[vmem, anywhere, smem, smem, anywhere, smem, vmem, vmem],
        out_specs=(anywhere, vmem),
        scratch_shapes=[
            pltpu.VMEM((nb, LANES, LANES), BF16),
            pltpu.VMEM((lo, ro, LANES), F32),
            pltpu.VMEM((lo, ro, LANES), F32),
            pltpu.VMEM((la, ra, LANES), F32),
            pltpu.VMEM((lo * CAP * ra, LANES), F32),
            pltpu.VMEM((8, LANES), I32),
            pltpu.VMEM((8, LANES), I32),
            pltpu.SMEM((8, LANES), I32),
            pltpu.VMEM((ngy, 1, LANES), F32),
            pltpu.VMEM((ngy, 1, LANES), F32),
            pltpu.VMEM((ngy, f_rows, LANES), BF16),
            pltpu.VMEM((ngy, f_rows, LANES), BF16),
            pltpu.VMEM((ro, ngy * 16), BF16),
            pltpu.VMEM((ngy // CHUNK, 4 * ro, CHUNK * 16), BF16),
            pltpu.VMEM((slots, ro), BF16),
            pltpu.VMEM((slots, 1, LANES), F32),
            pltpu.VMEM((slots, 1, LANES), F32),
            pltpu.VMEM((3, ro + 16, LANES), F32),
            pltpu.VMEM((3, ro, LANES), F32),
            dma,
            dma,
            dma,
            dma,
            dma,
            dma,
            dma,
            dma((ngy // CHUNK,)),
            dma,
            dma,
            *halo_scratch(ra, la),
            *halo_scratch(ro, 1),
            *halo_scratch(ro, lo - 1),
        ],
        compiler_params=pltpu.CompilerParams(
            collective_id=0, has_side_effects=True, vmem_limit_bytes=48 * 1024 * 1024
        ),
        cost_estimate=pl.CostEstimate(flops=200_000_000, bytes_accessed=5_000_000, transcendentals=100_000),
    )(atm_state, ocean_temp, flux_coef, flux_mix, share, src, dest, owner.reshape(1, nb))


def solution(mesh):
    ngy = mesh.shape["gy"]
    nx = 4
    return jax.shard_map(
        functools.partial(body, (mesh.shape["gx"], nx, ngy // nx)),
        mesh=mesh,
        in_specs=(
            P(None, "gx", "gy"),
            P(None, "gx", "gy"),
            P(),
            P(),
            P("gx", "gy", None, None),
            P("gx", "gy"),
            P("gx", "gy"),
            P("gx", "gy", None),
        ),
        out_specs=(P(None, "gx", "gy"), P("gx", "gy")),
        check_vma=False,
    )
```

time: 241 us -> 76.7 us (0.32)
  waiting for transfers between devices: 91.9 us -> 0 us
  starting transfers between devices: 85.6 us -> 0 us
  Pallas kernels: 0 us -> 66.9 us
  local copies, waits for them, and re-layouts: 30.6 us -> 8.81 us
  other arithmetic: 18.9 us -> 0 us
  matrix products: 10.7 us -> 0 us
    pallas_call x0 -> x1, Pallas kernels: none -> 66.9 us  [body(): pl.pallas_call(functools.partial(kernel, sizes), out_shape=(jax.ShapeDtyp...]
    all_to_all x3 -> x0, waiting for transfers between devices: 66.2 us -> none  [the longest x1 56.3 us: body(): lax.all_to_all(send_values, 'gy', split_axis=0, concat_axis=0, tiled=True)]
    ppermute x16 -> x0, starting transfers between devices: 51.7 us -> none  [the longest x8 31.7 us: with_halo(): lax.ppermute(lax.slice_in_dim(block, block.shape[dim] - width, None, axis...]
    all_to_all x3 -> x0, starting transfers between devices: 33.8 us -> none  [the longest x1 11.8 us: body(): lax.all_to_all(send_values, 'gy', split_axis=0, concat_axis=0, tiled=True)]
    ppermute x16 -> x0, waiting for transfers between devices: 25.8 us -> none  [the longest x8 16.5 us: with_halo(): lax.ppermute(lax.slice_in_dim(block, 0, width, axis=dim), axis, backward)]
    slice x13 -> x0, local copies, waits for them, and re-layouts: 11.2 us -> none  [the longest x10 7.87 us: with_halo(): lax.slice_in_dim(block, block.shape[dim] - width, None, axis=dim)]
    dot_general x7 -> x0, matrix products: 10.7 us -> none  [the longest x1 2.43 us: land_rows(): jnp.dot(tile_hit, flat, precision=lax.Precision.HIGHEST, preferred_elemen...]
    add x4 -> x0, other arithmetic: 9.13 us -> none  [diffuse_once(): return centre + diffusion_rate * (beside_all - 4.0 * centre)]
  transfers between devices with their start and end apart: 19 -> 0, of which waited for: 11 -> 0; matrix products, arithmetic and copies ran while one was open for 9% -> 0% of each run, Pallas kernels for 0% -> 0%
where the time goes in v1:
time: 76.7 us; the launch traced here: 76.4 us
  Pallas kernels  66.9 us (87%)
  local copies, waits for them, and re-layouts  8.81 us (11%)
    pallas_call x1, Pallas kernels, body(): pl.pallas_call(functools.partial(kernel, sizes), out_shape=(jax.ShapeDtyp...  66.9 us
    unnamed x17, local copies, waits for them, and re-layouts  8.81 us

profile of v1, /device:TPU:1, one launch (start us, length us, event | category | flops | bytes accessed | tf_op | source)
XLA Modules:
  0.0 76.4 jit_solution(15865629812096701084)
XLA Ops:
  0.6 0.8 %copy.10.coef_ref = f32[12,8]{1,0:T(8,128)S(1)} copy(f32[12,8]{0,1:T(8,128)} %param.10) | data formatting | bytes 768 | tf_op args[2]
  1.4 0.0 copy-start
  1.4 1.9 %copy-done = bf16[1,96,128,128]{3,2,1,0:T(8,128)(2,1)S(1)} copy-done((bf16[1,96,128,128]{3,2,1,0:T(8,128)(2,1)S(1)}, bf16[1,96,128,128]{3,2,1,0:T(8,128)(2,1)}, u32[]{:S(2)}) %copy-start) | copy-done | bytes 3145752
  3.3 0.0 copy-start.1
  3.3 1.1 %copy-done.1 = f32[10,128,128]{2,1,0:T(8,128)S(1)} copy-done((f32[10,128,128]{2,1,0:T(8,128)S(1)}, f32[10,128,128]{2,1,0:T(8,128)}, u32[]{:S(2)}) %copy-start.1) | copy-done | bytes 655384
  4.4 0.0 copy-start.2
  4.4 0.9 %copy-done.2 = f32[8,64,128]{2,1,0:T(8,128)S(1)} copy-done((f32[8,64,128]{2,1,0:T(8,128)S(1)}, f32[8,64,128]{2,1,0:T(8,128)}, u32[]{:S(2)}) %copy-start.2) | copy-done | bytes 262168
  5.3 0.0 copy-start.3
  5.3 0.7 copy-done.3
  6.0 0.0 copy-start.4
  6.0 0.7 copy-done.4
  6.7 0.0 copy-start.5
  6.7 0.7 copy-done.5
  7.3 0.0 copy-start.6
  7.3 0.7 copy-done.6
  8.0 66.9 %shard_map.95 = (f32[10,128,128]{2,1,0:T(8,128)S(1)}, f32[64,128]{1,0:T(8,128)S(1)}) custom-call(f32[8,64,128]{2,1,0:T(8,128)S(1)} %copy-done.2, f32[10,128,128]{2,1,0:T(8,128)S(1)} %copy-done.1, f32[12,8]{1,0:T(8,128)S(1)} %copy.10.coef_ref, f32[10,12]{1,0:T(8,128)S(1)} %copy-done.3, bf16[1,96,128,128]{3,2,1,0:T(8,128)(2,1)S(1)} %copy-done, ...), custom_call_target="tpu_custom_call" | custom-call | flops 200000000 | bytes 5000000 | tf_op jit(solution)/shard_map/pallas_call | solution.py:532
  74.9 0.8 %copy.13 = f32[10,128,128]{2,1,0:T(8,128)} copy(f32[10,128,128]{2,1,0:T(8,128)S(1)} %get-tuple-element.4) | data formatting | bytes 1310720
  75.7 0.6 copy.14
Async XLA Ops:
  1.4 1.9 %copy-start = (bf16[1,96,128,128]{3,2,1,0:T(8,128)(2,1)S(1)}, bf16[1,96,128,128]{3,2,1,0:T(8,128)(2,1)}, u32[]{:S(2)}) copy-start(bf16[1,96,128,128]{3,2,1,0:T(8,128)(2,1)} %share_hbm.1) | copy-start | bytes 9437188
  3.3 1.1 %copy-start.1 = (f32[10,128,128]{2,1,0:T(8,128)S(1)}, f32[10,128,128]{2,1,0:T(8,128)}, u32[]{:S(2)}) copy-start(f32[10,128,128]{2,1,0:T(8,128)} %ocean_hbm.1) | copy-start | bytes 1966084
  4.4 0.9 %copy-start.2 = (f32[8,64,128]{2,1,0:T(8,128)S(1)}, f32[8,64,128]{2,1,0:T(8,128)}, u32[]{:S(2)}) copy-start(f32[8,64,128]{2,1,0:T(8,128)} %atm_ref.1) | copy-start | bytes 786436
  5.3 0.7 copy-start.3
  6.0 0.7 copy-start.4
  6.7 0.7 copy-start.5
  7.3 0.7 copy-start.6

commit v2 on v1

--- a/solution.py
+++ b/solution.py
@@ -13,7 +13,11 @@
 F32, BF16, I32 = jnp.float32, jnp.bfloat16, jnp.int32
 LANES = 128
 NT = (((1,), (1,)), ((), ()))
-CHUNK = 16
+GROUP = 2
+SPAN = GROUP * CAP
+CHUNK = LANES // SPAN
+UNROLL = 4
+BURST = 8
 
 
 def iota(shape, dim):
@@ -35,18 +39,8 @@
         (self.top, self.bot, self.cl, self.cr, self.dg, self.ptl, self.ptr, self.pe, self.pk, self.ss, self.rs) = refs
         self.rows, self.count = rows, count
 
-    def start(self, field, packed):
+    def start(self, field, levels):
         rows = self.rows
-        tall = packed
-        if rows < LANES:
-            tall = jnp.concatenate([packed, jnp.zeros((LANES - rows, LANES), F32)], axis=0)
-        turned = tall.T
-        cs = self.ptl.shape[0]
-        self.ptl[...] = turned[0:cs]
-        self.ptr[...] = turned[64 : 64 + cs]
-        self.pe[0] = packed[0:8]
-        self.pe[1] = packed[rows - 8 : rows]
-        self.pk[...] = packed
         up, down = lax.rem(self.gx + self.ngx - 1, self.ngx), lax.rem(self.gx + 1, self.ngx)
         left, right = lax.rem(self.gy + self.ngy - 1, self.ngy), lax.rem(self.gy + 1, self.ngy)
         plan = (
@@ -70,7 +64,22 @@
             )
             for n, (src, dst, device) in enumerate(plan)
         ]
-        for copy in self.copies:
+        for copy in self.copies[0:2]:
+            copy.start()
+        packed = levels() if callable(levels) else levels
+        self.pe[0] = packed[0:8]
+        self.pe[1] = packed[rows - 8 : rows]
+        for copy in self.copies[4:8]:
+            copy.start()
+        tall = packed
+        if rows < LANES:
+            tall = jnp.concatenate([packed, jnp.zeros((LANES - rows, LANES), F32)], axis=0)
+        turned = tall.T
+        cs = self.ptl.shape[0]
+        self.ptl[...] = turned[0:cs]
+        self.ptr[...] = turned[64 : 64 + cs]
+        self.pk[...] = packed
+        for copy in self.copies[2:4]:
             copy.start()
 
     def arrive(self):
@@ -133,16 +142,22 @@
 
 def kernel(
     sizes,
+    atm_hbm,
+    ocean_hbm,
+    coef_hbm,
+    mix_hbm,
+    share_hbm,
+    src_hbm,
+    dest_hbm,
+    owner_hbm,
+    final_hbm,
+    aerial_ref,
     atm_ref,
-    ocean_hbm,
     coef_ref,
     mix_ref,
-    share_hbm,
     src_ref,
     dest_ref,
     owner_ref,
-    final_hbm,
-    aerial_ref,
     share,
     ocean,
     final,
@@ -160,10 +175,10 @@
     pick,
     s_send,
     s_recv,
+    home_lines,
     rims,
     mids,
-    share_sem,
-    ocean_sem,
+    in_sems,
     table_sem,
     final_sem,
     id_ss,
@@ -181,15 +196,28 @@
     la, ra = atm_ref.shape[0], atm_ref.shape[1]
     lo, ro = ocean.shape[0], ocean.shape[1]
     nb = src_ref.shape[1]
-    fluxes = coef_ref.shape[0]
+    fluxes = coef_ref.shape[1]
     gx, gy = lax.axis_index("gx"), lax.axis_index("gy")
     my_x, my_z = lax.div(gy, nz), lax.rem(gy, nz)
     place = (gx, gy, ngx, ngy)
 
-    share_copy = pltpu.make_async_copy(share_hbm.at[0], share, share_sem)
-    share_copy.start()
-    ocean_copy = pltpu.make_async_copy(ocean_hbm, ocean, ocean_sem)
-    ocean_copy.start()
+    loads = [
+        pltpu.make_async_copy(far, near, in_sems.at[n])
+        for n, (far, near) in enumerate(
+            (
+                (owner_hbm, owner_ref),
+                (dest_hbm, dest_ref),
+                (atm_hbm, atm_ref),
+                (coef_hbm, coef_ref),
+                (mix_hbm, mix_ref),
+                (src_hbm, src_ref),
+                (share_hbm.at[0], share),
+                (ocean_hbm, ocean),
+            )
+        )
+    ]
+    for load in loads:
+        load.start()
 
     def shift(i):
         k = lax.div(i, nx)
@@ -205,22 +233,30 @@
         dx, dz = shift(i)
         return lax.rem(my_x - dx + nx, nx) * nz + lax.rem(my_z - dz + nz, nz)
 
+    def to_all(act):
+        def burst(t, carry):
+            for u in range(BURST):
+                act(ngy - 1 - BURST * t - u)
+            return carry
+
+        lax.fori_loop(0, ngy // BURST - 1, burst, 0)
+        for i in reversed(range(1, BURST)):
+            act(i)
+
     barrier = pltpu.get_barrier_semaphore()
     up, down = lax.rem(gx + ngx - 1, ngx), lax.rem(gx + 1, ngx)
     left, right = lax.rem(gy + ngy - 1, ngy), lax.rem(gy + 1, ngy)
     for device in ((up, gy), (down, gy), (up, left), (up, right), (down, left), (down, right)):
         pl.semaphore_signal(barrier, inc=1, device_id=device, device_id_type=MESH)
 
-    def greet(i, carry):
-        pl.semaphore_signal(barrier, inc=1, device_id=(gx, ahead(i)), device_id_type=MESH)
-        return carry
-
-    lax.fori_loop(1, ngy, greet, 0)
+    to_all(lambda i: pl.semaphore_signal(barrier, inc=1, device_id=(gx, ahead(i)), device_id_type=MESH))
 
     atm_halo = Halo(place, halo_refs[0:11], ra, la)
     top_halo = Halo(place, halo_refs[11:22], ro, 1)
     low_halo = Halo(place, halo_refs[22:33], ro, lo - 1)
 
+    for load in loads[0:3]:
+        load.wait()
     lists[...] = jnp.full((8, LANES), -1, I32)
     lists[0:1, 0:nb] = owner_ref[...]
     lists[1:2, 0:nb] = dest_ref[...]
@@ -259,7 +295,7 @@
     for j in range(CAP):
         line = jnp.sum(jnp.where(slot_w == step_i * CAP + j, line_w, 0.0), axis=1, keepdims=True)
         ids = jnp.where(lax.rem(lane_i, CAP) == j, jnp.broadcast_to(line, wide), ids)
-    ids = jnp.where(lax.div(lane_i, 16) == lax.rem(step_i, 8), ids, 0.0)
+    ids = jnp.where(lax.div(lane_i, SPAN) == lax.rem(step_i, CHUNK), ids, 0.0)
     id_send[...] = ids.reshape(ngy, 1, LANES)
     id_recv[0] = id_send[0]
 
@@ -279,21 +315,17 @@
             device_id_type=MESH,
         )
 
-    def send_ids(i, carry):
-        id_copy(i).start()
-        return carry
-
-    lax.fori_loop(1, ngy, send_ids, 0)
+    to_all(lambda i: id_copy(i).start())
 
     atm_halo.arrive()
     rims[0, 0 : ra + 16] = atm_halo.rim
     mids[0, 0:ra] = atm_halo.mid
 
-    def atm_level(l, carry):
+    for l in range(la):
         surf[l] = atm_halo.two_steps(l, atm_ref[l], rims.at[0, 0 : ra + 16], mids.at[0, 0:ra])
-        return carry
-
-    lax.fori_loop(0, la, atm_level, 0)
+
+    for load in loads[3:5]:
+        load.wait()
 
     band = 16
 
@@ -302,9 +334,9 @@
         fields = [surf[l, pl.ds(r0, band)] for l in range(la)]
         flux = []
         for kk in range(fluxes):
-            total = coef_ref[kk, 0] * fields[0]
+            total = coef_ref[0, kk] * fields[0]
             for l in range(1, la):
-                total = total + coef_ref[kk, l] * fields[l]
+                total = total + coef_ref[l, kk] * fields[l]
             flux.append(jnp.tanh(total).astype(BF16).astype(F32))
         for l in range(lo):
             total = mix_ref[l, 0] * flux[0]
@@ -317,10 +349,10 @@
 
     lax.fori_loop(0, ra // band, flux_band, 0)
 
-    share_copy.wait()
     table_copy.wait()
-
-    f_rows = f_send.shape[1]
+    for load in loads[5:7]:
+        load.wait()
+
     used = lo * CAP
     slot_of_row = lax.rem(iota((used, LANES), 0), CAP)
 
@@ -341,7 +373,6 @@
             q = jnp.clip(table_s[1 + lax.div(s, LANES), lax.rem(s, LANES)], 0, nb - 1)
             rows = mixed[pl.ds(src_ref[0, q], used, stride=ra), :]
             rows = jnp.where(slot_of_row == j, rows, 0.0)
-            rows = jnp.concatenate([rows, jnp.zeros((f_rows - used, LANES), F32)], axis=0)
             left_parts.append(rows.astype(BF16))
             right_parts.append(share[q])
         return jnp.dot(
@@ -351,13 +382,19 @@
         ).astype(BF16)
 
     def send_blocks(t, carry):
-        i = ngy - 1 - t
-        f_send[i] = contribution(i)
+        last = ngy - 1 - UNROLL * t
+        steps = [last - u for u in range(UNROLL)]
+        for i, blocks in zip(steps, [contribution(i) for i in steps]):
+            f_send[i] = blocks
+            f_copy(i).start()
+        return carry
+
+    lax.fori_loop(0, ngy // UNROLL - 1, send_blocks, 0)
+    nearest = [contribution(i) for i in range(UNROLL)]
+    for i in reversed(range(1, UNROLL)):
+        f_send[i] = nearest[i]
         f_copy(i).start()
-        return carry
-
-    lax.fori_loop(0, ngy - 1, send_blocks, 0)
-    f_recv[0] = contribution(0)
+    f_recv[0] = nearest[0]
 
     pltpu.make_async_remote_copy(
         src_ref=id_send.at[1:ngy],
@@ -368,32 +405,29 @@
         device_id_type=MESH,
     ).wait_recv()
     line_of_row = iota((ro, LANES), 0) + 1
-    level_of_lane = lax.rem(lax.div(iota((ro, LANES), 1), CAP), CAP)
-    for g in range(ngy // 8):
-        ids_row = id_recv[8 * g]
-        for t in range(1, 8):
-            ids_row = ids_row + id_recv[8 * g + t]
+    level_of_lane = lax.rem(lax.div(iota((ro, LANES), 1), CAP), GROUP)
+    for c in range(chunks):
+        ids_row = id_recv[c * CHUNK]
+        for t in range(1, CHUNK):
+            ids_row = ids_row + id_recv[c * CHUNK + t]
         hit = jnp.where(jnp.broadcast_to(ids_row.astype(I32), (ro, LANES)) == line_of_row, 1.0, 0.0)
-        hits[:, g * LANES : (g + 1) * LANES] = hit.astype(BF16)
-        half = (g % 2) * LANES
-        for l in range(CAP):
-            spread[g // 2, l * ro : (l + 1) * ro, half : half + LANES] = jnp.where(
-                level_of_lane == l, hit, 0.0
-            ).astype(BF16)
-    chosen = iota((slots, ngy * 16), 0)
+        hits[:, c * LANES : (c + 1) * LANES] = hit.astype(BF16)
+        for l in range(GROUP):
+            spread[c, l * ro : (l + 1) * ro, :] = jnp.where(level_of_lane == l, hit, 0.0).astype(BF16)
+    chosen = iota((slots, ngy * SPAN), 0)
     chosen = jnp.where(
-        iota((slots, ngy * 16), 1) == lax.div(chosen, CAP) * 16 + lax.rem(chosen, CAP), 1.0, 0.0
+        iota((slots, ngy * SPAN), 1) == lax.div(chosen, CAP) * SPAN + lax.rem(chosen, CAP), 1.0, 0.0
     ).astype(BF16)
     pick[...] = lax.dot_general(chosen, hits[...], NT, preferred_element_type=F32).astype(BF16)
 
-    ocean_copy.wait()
+    loads[7].wait()
 
     def land(c, l0, l1):
-        base = 4 * (l0 // 4)
-        rows = f_recv[c * CHUNK : (c + 1) * CHUNK, base * CAP : base * CAP + 16, :]
+        base = GROUP * (l0 // GROUP)
+        rows = f_recv[c * CHUNK : (c + 1) * CHUNK, base * CAP : base * CAP + SPAN, :]
         landed = jnp.dot(
             spread[c, (l0 - base) * ro : (l1 - base) * ro, :],
-            rows.reshape(CHUNK * 16, LANES),
+            rows.reshape(LANES, LANES),
             preferred_element_type=F32,
         )
         for l in range(l0, l1):
@@ -411,14 +445,14 @@
             device_id_type=MESH,
         ).wait_recv()
         if c:
-            for l0 in range(0, lo, 4):
-                land(c, l0, min(lo, l0 + 4))
+            for l0 in range(0, lo, GROUP):
+                land(c, l0, l0 + GROUP)
     land(0, 0, 1)
-    top_halo.start(ocean.at[0:1], pack_sides([ocean[0]], ro))
-    land(0, 1, 4)
-    for l0 in range(4, lo, 4):
-        land(0, l0, min(lo, l0 + 4))
-    low_halo.start(ocean.at[1:lo], pack_sides([ocean[l] for l in range(1, lo)], ro))
+    top_halo.start(ocean.at[0:1], lambda: pack_sides([ocean[0]], ro))
+    land(0, 1, GROUP)
+    for l0 in range(GROUP, lo, GROUP):
+        land(0, l0, l0 + GROUP)
+    low_halo.start(ocean.at[1:lo], lambda: pack_sides([ocean[l] for l in range(1, lo)], ro))
 
     top_halo.arrive()
     rims[1] = top_halo.rim
@@ -426,25 +460,20 @@
     skin = top_halo.two_steps(0, ocean[0], rims.at[1], mids.at[1])
     final[0] = skin
     lines = jnp.dot(pick[...], skin.astype(BF16), preferred_element_type=F32)
-    s_send[...] = lines.reshape(slots, 1, LANES)
-    s_recv[0:CAP] = s_send[0:CAP]
+    s_send[...] = lines.reshape(ngy, CAP, LANES)
+    s_recv[0] = s_send[0]
 
     def s_copy(i):
-        here = pl.ds(i * CAP, CAP)
         return pltpu.make_async_remote_copy(
-            src_ref=s_send.at[here],
-            dst_ref=s_recv.at[here],
+            src_ref=s_send.at[i],
+            dst_ref=s_recv.at[i],
             send_sem=s_ss,
             recv_sem=s_rs,
             device_id=(gx, behind(i)),
             device_id_type=MESH,
         )
 
-    def send_lines(t, carry):
-        s_copy(ngy - 1 - t).start()
-        return carry
-
-    lax.fori_loop(0, ngy - 1, send_lines, 0)
+    to_all(lambda i: s_copy(i).start())
 
     low_halo.arrive()
     rims[2] = low_halo.rim
@@ -458,7 +487,7 @@
     final_copy = pltpu.make_async_copy(final, final_hbm, final_sem)
     final_copy.start()
 
-    rest = pl.ds(CAP, slots - CAP)
+    rest = pl.ds(1, ngy - 1)
     pltpu.make_async_remote_copy(
         src_ref=s_send.at[rest],
         dst_ref=s_recv.at[rest],
@@ -467,27 +496,31 @@
         device_id=(gx, gy),
         device_id_type=MESH,
     ).wait_recv()
+    home_lines[...] = s_recv[...].reshape(slots, 1, LANES)
     row_a = iota((ra, LANES), 0)
 
     def home(b, total):
+        return sum([part(b * UNROLL + u) for u in range(UNROLL)], total)
+
+    def part(b):
         left_parts, right_parts = [], []
         for j in range(4):
             q = b * 4 + j
-            line = jnp.broadcast_to(s_recv[jnp.clip(table_s[0, q], 0, slots - 1)], (ra, LANES))
+            line = jnp.broadcast_to(home_lines[jnp.clip(table_s[0, q], 0, slots - 1)], (ra, LANES))
             left_parts.append(jnp.where(row_a == src_ref[0, q], line, 0.0).astype(BF16))
             right_parts.append(share[q])
-        return total + lax.dot_general(
+        return lax.dot_general(
             jnp.concatenate(left_parts, axis=1),
             jnp.concatenate(right_parts, axis=1),
             NT,
             preferred_element_type=F32,
         )
 
-    aerial_ref[...] = lax.fori_loop(0, nb // 4, home, jnp.zeros((ra, LANES), F32))
+    aerial_ref[...] = lax.fori_loop(0, nb // (4 * UNROLL), home, jnp.zeros((ra, LANES), F32))
 
     for halo in (atm_halo, top_halo, low_halo):
         halo.wait_sent()
-    for buffer, sem, first in ((id_send, id_ss, 1), (f_send, f_ss, 1), (s_send, s_ss, CAP)):
+    for buffer, sem, first in ((id_send, id_ss, 1), (f_send, f_ss, 1), (s_send, s_ss, 1)):
         here = pl.ds(first, buffer.shape[0] - first)
         pltpu.make_async_remote_copy(
             src_ref=buffer.at[here],
@@ -524,10 +557,8 @@
     la, ra, _ = atm_state.shape
     lo, ro, _ = ocean_temp.shape
     nb = src.shape[1]
-    f_rows = -(-lo * CAP // 16) * 16
     vmem = pl.BlockSpec(memory_space=pltpu.VMEM)
-    smem = pl.BlockSpec(memory_space=pltpu.SMEM)
-    anywhere = pl.BlockSpec(memory_space=pl.ANY)
+    far = pl.BlockSpec(memory_space=pltpu.HBM)
     dma = pltpu.SemaphoreType.DMA
     return pl.pallas_call(
         functools.partial(kernel, sizes),
@@ -535,9 +566,15 @@
             jax.ShapeDtypeStruct(ocean_temp.shape, F32),
             jax.ShapeDtypeStruct((ra, LANES), F32),
         ),
-        in_specs=[vmem, anywhere, smem, smem, anywhere, smem, vmem, vmem],
-        out_specs=(anywhere, vmem),
+        in_specs=[far] * 8,
+        out_specs=(far, vmem),
         scratch_shapes=[
+            pltpu.VMEM(atm_state.shape, F32),
+            pltpu.SMEM(flux_coef.shape[::-1], F32),
+            pltpu.SMEM(flux_mix.shape, F32),
+            pltpu.SMEM((1, nb), I32),
+            pltpu.VMEM((1, nb), I32),
+            pltpu.VMEM((1, nb), I32),
             pltpu.VMEM((nb, LANES, LANES), BF16),
             pltpu.VMEM((lo, ro, LANES), F32),
             pltpu.VMEM((lo, ro, LANES), F32),
@@ -548,17 +585,17 @@
             pltpu.SMEM((8, LANES), I32),
             pltpu.VMEM((ngy, 1, LANES), F32),
             pltpu.VMEM((ngy, 1, LANES), F32),
-            pltpu.VMEM((ngy, f_rows, LANES), BF16),
-            pltpu.VMEM((ngy, f_rows, LANES), BF16),
-            pltpu.VMEM((ro, ngy * 16), BF16),
-            pltpu.VMEM((ngy // CHUNK, 4 * ro, CHUNK * 16), BF16),
+            pltpu.VMEM((ngy, lo * CAP, LANES), BF16),
+            pltpu.VMEM((ngy, lo * CAP, LANES), BF16),
+            pltpu.VMEM((ro, ngy * SPAN), BF16),
+            pltpu.VMEM((ngy // CHUNK, GROUP * ro, LANES), BF16),
             pltpu.VMEM((slots, ro), BF16),
-            pltpu.VMEM((slots, 1, LANES), F32),
+            pltpu.VMEM((ngy, CAP, LANES), F32),
+            pltpu.VMEM((ngy, CAP, LANES), F32),
             pltpu.VMEM((slots, 1, LANES), F32),
             pltpu.VMEM((3, ro + 16, LANES), F32),
             pltpu.VMEM((3, ro, LANES), F32),
-            dma,
-            dma,
+            dma((8,)),
             dma,
             dma,
             dma,
@@ -572,10 +609,10 @@
             *halo_scratch(ro, lo - 1),
         ],
         compiler_params=pltpu.CompilerParams(
-            collective_id=0, has_side_effects=True, vmem_limit_bytes=48 * 1024 * 1024
+            collective_id=0, has_side_effects=True, vmem_limit_bytes=60 * 1024 * 1024
         ),
         cost_estimate=pl.CostEstimate(flops=200_000_000, bytes_accessed=5_000_000, transcendentals=100_000),
-    )(atm_state, ocean_temp, flux_coef, flux_mix, share, src, dest, owner.reshape(1, nb))
+    )(atm_state, ocean_temp, flux_coef.T, flux_mix, share, src, dest, owner.reshape(1, nb))
 
 
 def solution(mesh):

time: 76.7 us -> 63.2 us (0.82)
  Pallas kernels: 66.9 us -> 59 us
  local copies, waits for them, and re-layouts: 8.81 us -> 3.35 us
    pallas_call x1, Pallas kernels: 66.9 us -> 59 us  [body(): pl.pallas_call(functools.partial(kernel, sizes), out_shape=(jax.ShapeDtyp...]
    unnamed x17 -> x2, local copies, waits for them, and re-layouts: 8.81 us -> 3.35 us
where the time goes in v2:
time: 63.2 us; the launch traced here: 63 us
  Pallas kernels  59 us (93%)
  local copies, waits for them, and re-layouts  3.35 us (5%)
  between operations  0.64 us (1%)
    pallas_call x1, Pallas kernels, body(): pl.pallas_call(functools.partial(kernel, sizes), out_shape=(jax.ShapeDtyp...  59 us
    unnamed x2, local copies, waits for them, and re-layouts  3.35 us

profile of v2, /device:TPU:1, one launch (start us, length us, event | category | flops | bytes accessed | tf_op | source)
XLA Modules:
  0.0 63.0 jit_solution(8857023327758722519)
XLA Ops:
  0.6 59.0 %shard_map.95 = (f32[10,128,128]{2,1,0:T(8,128)}, f32[64,128]{1,0:T(8,128)}) custom-call(f32[8,64,128]{2,1,0:T(8,128)} %atm_hbm.1, f32[10,128,128]{2,1,0:T(8,128)} %ocean_hbm.1, f32[8,12]{1,0:T(8,128)} %bitcast.2, f32[10,12]{1,0:T(8,128)} %mix_hbm.1, bf16[1,96,128,128]{3,2,1,0:T(8,128)(2,1)} %share_hbm.1, s32[1,96]{1,0:T(1,128)} %src_hbm.1, ...), custom_call_target="tpu_custom_call" | custom-call | flops 200000000 | bytes 5000000 | tf_op jit(solution)/shard_map/pallas_call | solution.py:563
  59.6 2.0 %copy.12 = f32[10,128,128]{2,1,0:T(8,128)} copy(f32[10,128,128]{2,1,0:T(8,128)} %get-tuple-element.4) | data formatting | bytes 1310720
  61.6 1.4 %copy.13 = f32[64,128]{1,0:T(8,128)} copy(f32[64,128]{1,0:T(8,128)} %get-tuple-element.5) | data formatting | bytes 65536

commit v3 on v2

--- a/solution.py
+++ b/solution.py
@@ -105,7 +105,10 @@
         near = sides + self.pk[...]
         beside = jnp.where(low, pltpu.roll(near, 1, 1), pltpu.roll(near, LANES - 1, 1))
         mid = sides + RATE * (up + down + beside - 4.0 * sides)
-        self.rim, self.mid = rim, jnp.where(edge, mid, 0.0)
+        mid = jnp.where(edge, mid, 0.0)
+        odd = lax.rem(lane, 2) == 1
+        self.rim = jnp.where(odd, rim, pltpu.roll(rim, 64, 1))
+        self.mid = jnp.where(odd, mid, pltpu.roll(mid, 64, 1))
 
     def two_steps(self, n, field, rim_ref, mid_ref):
         rows = self.rows
@@ -115,10 +118,11 @@
         bot = jnp.where(self.has_bot, self.bot[n], 0.0)
         whole = jnp.concatenate([top, field, bot], axis=0)
         lane, row = iota((total, LANES), 1), iota((total, LANES), 0)
-        to_first, to_last = LANES - 1 - 2 * n, 63 - 2 * n
+        to_ends = LANES - 1 - 2 * n
+        side = pltpu.roll(rim, to_ends, 1)
         beside = (
-            jnp.where(lane == 0, pltpu.roll(rim, to_first, 1), pltpu.roll(whole, 1, 1))
-            + jnp.where(lane == LANES - 1, pltpu.roll(rim, to_last, 1), pltpu.roll(whole, LANES - 1, 1))
+            jnp.where(lane == 0, side, pltpu.roll(whole, 1, 1))
+            + jnp.where(lane == LANES - 1, side, pltpu.roll(whole, LANES - 1, 1))
             + pltpu.roll(whole, 1, 0)
             + pltpu.roll(whole, total - 1, 0)
         )
@@ -127,9 +131,10 @@
         mid = jnp.where((row >= first_row) & (row < last_row), mid, 0.0)
         own = mid[8 : rows + 8]
         lane = iota((rows, LANES), 1)
+        side = pltpu.roll(rim_mid, to_ends, 1)
         beside = (
-            jnp.where(lane == 0, pltpu.roll(rim_mid, to_first, 1), pltpu.roll(own, 1, 1))
-            + jnp.where(lane == LANES - 1, pltpu.roll(rim_mid, to_last, 1), pltpu.roll(own, LANES - 1, 1))
+            jnp.where(lane == 0, side, pltpu.roll(own, 1, 1))
+            + jnp.where(lane == LANES - 1, side, pltpu.roll(own, LANES - 1, 1))
             + pltpu.roll(mid, 1, 0)[8 : rows + 8]
             + pltpu.roll(mid, total - 1, 0)[8 : rows + 8]
         )
@@ -479,11 +484,8 @@
     rims[2] = low_halo.rim
     mids[2] = low_halo.mid
 
-    def low_level(n, carry):
+    for n in range(lo - 1):
         final[n + 1] = low_halo.two_steps(n, ocean[n + 1], rims.at[2], mids.at[2])
-        return carry
-
-    lax.fori_loop(0, lo - 1, low_level, 0)
     final_copy = pltpu.make_async_copy(final, final_hbm, final_sem)
     final_copy.start()
 
@@ -609,10 +611,15 @@
             *halo_scratch(ro, lo - 1),
         ],
         compiler_params=pltpu.CompilerParams(
-            collective_id=0, has_side_effects=True, vmem_limit_bytes=60 * 1024 * 1024
+            collective_id=0, has_side_effects=True, vmem_limit_bytes=48 * 1024 * 1024
         ),
         cost_estimate=pl.CostEstimate(flops=200_000_000, bytes_accessed=5_000_000, transcendentals=100_000),
-    )(atm_state, ocean_temp, flux_coef.T, flux_mix, share, src, dest, owner.reshape(1, nb))
+    )(
+        *(
+            pltpu.with_memory_space_constraint(x, pltpu.HBM)
+            for x in (atm_state, ocean_temp, flux_coef.T, flux_mix, share, src, dest, owner.reshape(1, nb))
+        )
+    )
 
 
 def solution(mesh):

time: 63.2 us -> 60.4 us (0.956)
  local copies, waits for them, and re-layouts: 3.35 us -> 1.45 us
  Pallas kernels: 59 us -> 58.1 us
    unnamed x2, local copies, waits for them, and re-layouts: 3.35 us -> 1.45 us
    pallas_call x1, Pallas kernels: 59 us -> 58.1 us  [body(): pl.pallas_call(functools.partial(kernel, sizes), out_shape=(jax.ShapeDtyp...]
where the time goes in v3:
time: 60.4 us; the launch traced here: 60.2 us
  Pallas kernels  58.1 us (96%)
  local copies, waits for them, and re-layouts  1.45 us (2%)
  between operations  0.64 us (1%)
    pallas_call x1, Pallas kernels, body(): pl.pallas_call(functools.partial(kernel, sizes), out_shape=(jax.ShapeDtyp...  58.1 us
    unnamed x2, local copies, waits for them, and re-layouts  1.45 us

profile of v3, /device:TPU:1, one launch (start us, length us, event | category | flops | bytes accessed | tf_op | source)
XLA Modules:
  0.0 60.2 jit_solution(6137577487882226490)
XLA Ops:
  0.6 58.1 %shard_map.95 = (f32[10,128,128]{2,1,0:T(8,128)S(1)}, f32[64,128]{1,0:T(8,128)S(1)}) custom-call(f32[8,64,128]{2,1,0:T(8,128)} %atm_hbm.1, f32[10,128,128]{2,1,0:T(8,128)} %ocean_hbm.1, f32[8,12]{1,0:T(8,128)} %bitcast.2, f32[10,12]{1,0:T(8,128)} %mix_hbm.1, bf16[1,96,128,128]{3,2,1,0:T(8,128)(2,1)} %share_hbm.1, s32[1,96]{1,0:T(1,128)} %src_hbm.1, ...), custom_call_target="tpu_custom_call" | custom-call | flops 200000000 | bytes 5000000 | tf_op jit(solution)/shard_map/pallas_call | solution.py:565
  58.8 0.8 %copy.12 = f32[10,128,128]{2,1,0:T(8,128)} copy(f32[10,128,128]{2,1,0:T(8,128)S(1)} %get-tuple-element.4) | data formatting | bytes 1310720
  59.6 0.6 %copy.13 = f32[64,128]{1,0:T(8,128)} copy(f32[64,128]{1,0:T(8,128)S(1)} %get-tuple-element.5) | data formatting | bytes 65536

commit v4 on v3

--- a/solution.py
+++ b/solution.py
@@ -465,7 +465,7 @@
     skin = top_halo.two_steps(0, ocean[0], rims.at[1], mids.at[1])
     final[0] = skin
     lines = jnp.dot(pick[...], skin.astype(BF16), preferred_element_type=F32)
-    s_send[...] = lines.reshape(ngy, CAP, LANES)
+    s_send[...] = lines.astype(BF16).reshape(ngy, CAP, LANES)
     s_recv[0] = s_send[0]
 
     def s_copy(i):
@@ -498,7 +498,7 @@
         device_id=(gx, gy),
         device_id_type=MESH,
     ).wait_recv()
-    home_lines[...] = s_recv[...].reshape(slots, 1, LANES)
+    home_lines[...] = s_recv[...].astype(F32).reshape(slots, 1, LANES)
     row_a = iota((ra, LANES), 0)
 
     def home(b, total):
@@ -592,8 +592,8 @@
             pltpu.VMEM((ro, ngy * SPAN), BF16),
             pltpu.VMEM((ngy // CHUNK, GROUP * ro, LANES), BF16),
             pltpu.VMEM((slots, ro), BF16),
-            pltpu.VMEM((ngy, CAP, LANES), F32),
-            pltpu.VMEM((ngy, CAP, LANES), F32),
+            pltpu.VMEM((ngy, CAP, LANES), BF16),
+            pltpu.VMEM((ngy, CAP, LANES), BF16),
             pltpu.VMEM((slots, 1, LANES), F32),
             pltpu.VMEM((3, ro + 16, LANES), F32),
             pltpu.VMEM((3, ro, LANES), F32),

time: 60.4 us -> 60.2 us (level)
  no operation moved by 1% of the time
where the time goes in v4:
time: 60.2 us; the launch traced here: 60.1 us
  Pallas kernels  58 us (96%)
  local copies, waits for them, and re-layouts  1.45 us (2%)
  between operations  0.64 us (1%)
    pallas_call x1, Pallas kernels, body(): pl.pallas_call(functools.partial(kernel, sizes), out_shape=(jax.ShapeDtyp...  58 us
    unnamed x2, local copies, waits for them, and re-layouts  1.45 us

profile of v4, /device:TPU:1, one launch (start us, length us, event | category | flops | bytes accessed | tf_op | source)
XLA Modules:
  0.0 60.1 jit_solution(12934313029132139924)
XLA Ops:
  0.6 58.0 %shard_map.95 = (f32[10,128,128]{2,1,0:T(8,128)S(1)}, f32[64,128]{1,0:T(8,128)S(1)}) custom-call(f32[8,64,128]{2,1,0:T(8,128)} %atm_hbm.1, f32[10,128,128]{2,1,0:T(8,128)} %ocean_hbm.1, f32[8,12]{1,0:T(8,128)} %bitcast.2, f32[10,12]{1,0:T(8,128)} %mix_hbm.1, bf16[1,96,128,128]{3,2,1,0:T(8,128)(2,1)} %share_hbm.1, s32[1,96]{1,0:T(1,128)} %src_hbm.1, ...), custom_call_target="tpu_custom_call" | custom-call | flops 200000000 | bytes 5000000 | tf_op jit(solution)/shard_map/pallas_call | solution.py:565
  58.6 0.8 %copy.12 = f32[10,128,128]{2,1,0:T(8,128)} copy(f32[10,128,128]{2,1,0:T(8,128)S(1)} %get-tuple-element.4) | data formatting | bytes 1310720
  59.5 0.6 %copy.13 = f32[64,128]{1,0:T(8,128)} copy(f32[64,128]{1,0:T(8,128)S(1)} %get-tuple-element.5) | data formatting | bytes 65536
